TPU v7x, 512 devices: a whole 4x8x8 slice. The times are simulated.
512 devices in a mesh: row: 32 (over y_lo, x, core), col: 16 (over z, y_hi).
Axes of the slice: x: 4, y: 8 (y_hi: 2, y_lo: 4; y = y_hi * 4 + y_lo), z: 8, core: 2. Of those that a mesh axis runs over, the one named last changes fastest.
Arguments:
- noise: bfloat16 [256, 65536], P('row', 'col')
- data: bfloat16 [512, 65536], P('col', 'row'), may hold values from -6 to 6
- noise_weight: int32 [256], P('row'), may hold values from 1 to 8, as said below
- data_weight: int32 [512], P('col'), may hold values from 1 to 8, as said below
Outputs:
- targets: bfloat16 [256, 65536], P('row', 'col')
- noise_potential: float32 [256], P('row')
- data_potential: float32 [512], P('col')
Inputs may be any that keep to these rules, and one draw needn't show every extreme that they name: `noise_weight`: weights rise in range with the sample index; the last sample has weight 8. `data_weight`: weights rise in range with the sample index; the last sample has weight 8.
All inputs are finite; a program needn't handle non-finite values.
Results may differ from a plain program's by a relative error of at most 0.025.
Values may be sent and summed in bfloat16 or wider, within the bound.
A program may use at most 64 MiB of HBM per device.

v0:
```python
import math

import jax
import jax.numpy as jnp
from jax import lax
from jax.sharding import PartitionSpec as P

HALVES = 4


def lse_over_data(scores):
    local_peak = jnp.max(scores, axis=1)
    peak = lax.pmax(local_peak, "col")
    total = lax.psum(jnp.sum(jnp.exp(scores - peak[:, None]), axis=1), "col")
    return peak + jnp.log(total)


def lse_over_noise(scores):
    local_peak = jnp.max(scores, axis=0)
    peak = lax.pmax(local_peak, "row")
    total = lax.psum(jnp.sum(jnp.exp(scores - peak[None, :]), axis=0), "row")
    return peak + jnp.log(total)


def per_device(noise, data, noise_weight, data_weight):
    width = noise.shape[1] * lax.axis_size("col")
    eps = 1.0 / math.sqrt(width)
    noise_full = lax.all_gather(noise, "col", axis=1, tiled=True)
    noise_sq = jnp.einsum("nf,nf->n", noise_full, noise_full, preferred_element_type=jnp.float32)
    data_full = lax.all_gather(data, "row", axis=1, tiled=True)
    data_sq = jnp.einsum("nf,nf->n", data_full, data_full, preferred_element_type=jnp.float32)
    cross = jnp.dot(noise_full, data_full.T, preferred_element_type=jnp.float32)
    cost = (noise_sq[:, None] + data_sq[None, :] - 2.0 * cross) / width
    noise_mass = lax.psum(jnp.sum(noise_weight.astype(jnp.float32)), "row")
    data_mass = lax.psum(jnp.sum(data_weight.astype(jnp.float32)), "col")
    log_a = jnp.log(noise_weight.astype(jnp.float32) / noise_mass)
    log_b = jnp.log(data_weight.astype(jnp.float32) / data_mass)
    data_pot = jnp.zeros((data.shape[0],), jnp.float32)
    noise_pot = jnp.zeros((noise.shape[0],), jnp.float32)
    for rounds in range(HALVES // 2):
        noise_pot = eps * log_a - eps * lse_over_data((data_pot[None, :] - cost) / eps)
        data_pot = eps * log_b - eps * lse_over_noise((noise_pot[:, None] - cost) / eps)
    plan = jnp.exp((noise_pot[:, None] + data_pot[None, :] - cost) / eps)
    mass = lax.psum(jnp.sum(plan, axis=1), "col")
    plan_low = plan.astype(jnp.bfloat16)
    partial_value = jnp.dot(plan_low, data_full, preferred_element_type=jnp.float32)
    summed = lax.psum_scatter(
        partial_value.astype(jnp.bfloat16), "col", scatter_dimension=1, tiled=True
    ).astype(jnp.float32)
    targets = (summed / mass[:, None]).astype(jnp.bfloat16)
    return (targets, noise_pot, data_pot)


def solution(mesh):
    placed = (P("row", "col"), P("col", "row"), P("row"), P("col"))
    return jax.shard_map(
        per_device,
        mesh=mesh,
        in_specs=placed,
        out_specs=(P("row", "col"), P("row"), P("col")),
        check_vma=False,
    )
```

profile of v0, /device:TPU:1, one launch (start us, length us, event | category | flops | bytes accessed | tf_op | source)
XLA Modules:
  0.0 938.9 jit_solution(17018136701896003151)
XLA Ops:
  7.2 0.0 all-gather.3.cloned.1.call-start
  7.2 0.7 all-gather.3.cloned.1.call-update
  7.9 0.0 all-gather.5.cloned.1.call-start
  7.9 0.7 all-gather.5.cloned.1.call-update
  8.6 0.0 reduce-scatter.2.cloned.1.call-start
  8.7 1.3 convert_reduce_fusion
  10.0 1.3 convert_reduce_fusion.1
  11.2 90.7 %all-gather.3.cloned.1.call-done = bf16[8,65536]{1,0:T(8,128)(2,1)} async-done(((bf16[8,4096]{1,0:T(8,128)(2,1)}), bf16[8,65536]{1,0:T(8,128)(2,1)}) %all-gather.3.cloned.1.call-update) | async-done | bytes 1048592 | tf_op jit(solution)/shard_map/all_gather | solution.py:28
  101.9 0.0 copy-start.1
  101.9 2.0 fusion.1
  103.9 0.0 copy-start.4
  103.9 67.0 %all-gather.5.cloned.1.call-done = bf16[32,65536]{1,0:T(8,128)(2,1)} async-done(((bf16[32,2048]{1,0:T(8,128)(2,1)}), bf16[32,65536]{1,0:T(8,128)(2,1)}) %all-gather.5.cloned.1.call-update) | async-done | bytes 4194320 | tf_op jit(solution)/shard_map/all_gather | solution.py:30
  170.9 0.0 copy-start
  170.9 0.0 copy-start.5
  170.9 3.3 fusion
  174.2 0.0 copy-done.1
  174.2 0.2 copy-done
  174.4 1.3 fusion.4
  175.7 46.6 %pmax.28 = f32[8]{0:T(128)S(1)} all-reduce(f32[8]{0:T(128)S(1)} %get-tuple-element.9), channel_id=1, replica_groups=mesh['row'=32,'col'=16] {'col'}, use_global_device_ids=true, to_apply=%region_5.0 | all-reduce | flops 8 | bytes 64 | tf_op jit(solution)/shard_map/pmax | solution.py:13
  222.2 0.2 exponential_reduce_fusion.3
  222.4 74.9 %psum.49 = f32[]{:T(128)} all-reduce(f32[]{:T(128)} %convert_reduce_fusion.1), channel_id=1, replica_groups=mesh['row'=32,'col'=16] {'row'}, use_global_device_ids=true, to_apply=%region_1.0 | all-reduce | flops 1 | bytes 8 | tf_op jit(solution)/shard_map/psum | solution.py:34
  297.3 40.1 %all-reduce = (f32[]{:T(128)}, f32[8]{0:T(128)S(1)}) all-reduce(f32[]{:T(128)} %convert_reduce_fusion, f32[8]{0:T(128)S(1)} %exponential_reduce_fusion.3), channel_id=1, replica_groups=mesh['row'=32,'col'=16] {'col'}, use_global_device_ids=true, to_apply=%region_3.0 | all-reduce | flops 9 | bytes 72 | tf_op jit(solution)/shard_map/psum | solution.py:35
  337.4 0.0 copy-done.4
  337.4 0.7 multiply_subtract_fusion.3
  338.0 0.1 fusion.5
  338.1 74.3 %pmax.29 = f32[32]{0:T(128)S(1)} all-reduce(f32[32]{0:T(128)S(1)} %fusion.5), channel_id=1, replica_groups=mesh['row'=32,'col'=16] {'row'}, use_global_device_ids=true, to_apply=%region_9.0 | all-reduce | flops 32 | bytes 256 | tf_op jit(solution)/shard_map/pmax | solution.py:20
  412.4 0.1 exponential_reduce_fusion.2
  412.5 67.4 %psum.52 = f32[32]{0:T(128)S(1)} all-reduce(f32[32]{0:T(128)S(1)} %exponential_reduce_fusion.2), channel_id=1, replica_groups=mesh['row'=32,'col'=16] {'row'}, use_global_device_ids=true, to_apply=%region_11.0 | all-reduce | flops 32 | bytes 256 | tf_op jit(solution)/shard_map/psum | solution.py:21
  479.9 0.0 copy-done.5
  479.9 0.7 multiply_subtract_fusion.2
  480.6 0.1 fusion.6
  480.7 45.2 %pmax.30 = f32[8]{0:T(128)S(1)} all-reduce(f32[8]{0:T(128)S(1)} %fusion.6), channel_id=1, replica_groups=mesh['row'=32,'col'=16] {'col'}, use_global_device_ids=true, to_apply=%region_13.0 | all-reduce | flops 8 | bytes 64 | tf_op jit(solution)/shard_map/pmax | solution.py:13
  525.8 0.2 exponential_reduce_fusion.1
  526.0 39.5 %psum.53 = f32[8]{0:T(128)S(1)} all-reduce(f32[8]{0:T(128)S(1)} %exponential_reduce_fusion.1), channel_id=1, replica_groups=mesh['row'=32,'col'=16] {'col'}, use_global_device_ids=true, to_apply=%region_15.0 | all-reduce | flops 8 | bytes 64 | tf_op jit(solution)/shard_map/psum | solution.py:14
  565.5 0.0 copy-start.2
  565.5 0.1 fusion.7
  565.6 81.5 %pmax.31 = f32[32]{0:T(128)S(1)} all-reduce(f32[32]{0:T(128)S(1)} %fusion.7), channel_id=1, replica_groups=mesh['row'=32,'col'=16] {'row'}, use_global_device_ids=true, to_apply=%region_17.0 | all-reduce | flops 32 | bytes 256 | tf_op jit(solution)/shard_map/pmax | solution.py:20
  647.1 0.1 exponential_reduce_fusion
  647.2 67.4 %psum.54 = f32[32]{0:T(128)S(1)} all-reduce(f32[32]{0:T(128)S(1)} %exponential_reduce_fusion), channel_id=1, replica_groups=mesh['row'=32,'col'=16] {'row'}, use_global_device_ids=true, to_apply=%region_19.0 | all-reduce | flops 32 | bytes 256 | tf_op jit(solution)/shard_map/psum | solution.py:21
  714.7 0.0 copy-start.3
  714.7 3.9 convolution_convert_fusion
  718.6 0.0 reduce-scatter.2.cloned.1.call-update
  718.6 0.2 fusion.8
  718.8 45.2 %psum.55 = f32[8]{0:T(128)S(1)} all-reduce(f32[8]{0:T(128)S(1)} %fusion.8), channel_id=1, replica_groups=mesh['row'=32,'col'=16] {'col'}, use_global_device_ids=true, to_apply=%region_22.0 | all-reduce | flops 8 | bytes 64 | tf_op jit(solution)/shard_map/psum | solution.py:44
  763.9 166.9 %reduce-scatter.2.cloned.1.call-done = bf16[8,4096]{1,0:T(8,128)(2,1)} async-done(((bf16[8,65536]{1,0:T(8,128)(2,1)}), bf16[8,4096]{1,0:T(8,128)(2,1)}) %reduce-scatter.2.cloned.1.call-update) | async-done | bytes 65552 | tf_op jit(solution)/shard_map/reduce_scatter | solution.py:47
  930.8 1.5 divide_convert_fusion
  932.3 0.0 copy-done.2
  932.3 0.0 copy-done.3
  (2 shorter events, 0.0 us)
Async XLA Ops:
  7.2 94.8 %all-gather.3.cloned.1.call-start = ((), (), s32[]{:S(2)}) async-start(), calls=%async_computation.1 | async-start | bytes 1114112 | tf_op jit(solution)/shard_map/all_gather | solution.py:28
  7.9 163.0 %all-gather.5.cloned.1.call-start = ((), (), s32[]{:S(2)}) async-start(), calls=%async_computation.2 | async-start | bytes 4325376 | tf_op jit(solution)/shard_map/all_gather | solution.py:30
  8.6 922.1 %reduce-scatter.2.cloned.1.call-start = ((), (), s32[]{:S(2)}) async-start(), calls=%async_computation.3 | async-start | bytes 1114112 | tf_op jit(solution)/shard_map/reduce_scatter | solution.py:47
  101.9 72.2 %copy-start.1 = (bf16[8,65536]{1,0:T(8,128)(2,1)S(1)}, bf16[8,65536]{1,0:T(8,128)(2,1)}, u32[]{:S(2)}) copy-start(bf16[8,65536]{1,0:T(8,128)(2,1)} %all-gather.3.cloned.1.call-done) | copy-start | bytes 3145732
  103.9 233.5 %copy-start.4 = (s32[8]{0:T(128)S(1)}, s32[8]{0:T(128)}, u32[]{:S(2)}) copy-start(s32[8]{0:T(128)} %param.6) | copy-start | bytes 100
  170.9 3.4 copy-start
  170.9 309.0 %copy-start.5 = (s32[32]{0:T(128)S(1)}, s32[32]{0:T(128)}, u32[]{:S(2)}) copy-start(s32[32]{0:T(128)} %param.7) | copy-start | bytes 388
  565.5 366.8 %copy-start.2 = (f32[8]{0:T(128)}, f32[8]{0:T(128)S(1)}, u32[]{:S(2)}) copy-start(f32[8]{0:T(128)S(1)} %multiply_subtract_fusion.1) | copy-start | bytes 100
  714.7 217.7 %copy-start.3 = (f32[32]{0:T(128)}, f32[32]{0:T(128)S(1)}, u32[]{:S(2)}) copy-start(f32[32]{0:T(128)S(1)} %multiply_subtract_fusion) | copy-start | bytes 388
Sparse Core Ops, SparseCore 0:
  11.2 90.7 all-gather.2
  104.1 66.7 all-gather.4
  718.7 212.0 reduce-scatter.1
where the time goes:
time: 944 us; the launch traced here: 939 us
  blocking collectives  582 us (62%)
  waiting for transfers between devices  326 us (35%)
  between operations  13.8 us (1%)
  other arithmetic  11.6 us (1%)
    reduce_scatter x1, waiting for transfers between devices, per_device(): lax.psum_scatter(partial_value.astype(jnp.bfloat16), 'col', scatter_dimen...  167 us
    pmax x2, blocking collectives, lse_over_noise(): peak = lax.pmax(local_peak, 'row')  156 us
    psum x2, blocking collectives, lse_over_noise(): total = lax.psum(jnp.sum(jnp.exp(scores - peak[None, :]), axis=0), 'row')  135 us
    pmax x2, blocking collectives, lse_over_data(): peak = lax.pmax(local_peak, 'col')  91.7 us
    all_gather x1, waiting for transfers between devices, per_device(): noise_full = lax.all_gather(noise, 'col', axis=1, tiled=True)  90.7 us
    psum x1, blocking collectives, per_device(): noise_mass = lax.psum(jnp.sum(noise_weight.astype(jnp.float32)), 'row')  74.9 us
    all_gather x1, waiting for transfers between devices, per_device(): data_full = lax.all_gather(data, 'row', axis=1, tiled=True)  67 us
    psum x1, blocking collectives, per_device(): mass = lax.psum(jnp.sum(plan, axis=1), 'col')  45.2 us
  transfers between devices with their start and end apart: 3, of which 3 were waited for; matrix products, arithmetic and copies ran while one was open for 0% of the time, Pallas kernels for 0%

commit v1 on v0

v1 whole, which is shorter than its diff:
```python
import functools
import math

import jax
import jax.numpy as jnp
from jax import lax
from jax.experimental import pallas as pl
from jax.experimental.pallas import tpu as pltpu
from jax.sharding import PartitionSpec as P

HALVES = 4
MESH = pl.DeviceIdType.MESH
F32 = jnp.float32
BF16 = jnp.bfloat16
LANES = 128


def kernel(
    Q, C, width,
    nw_ref, dw_ref, noise_ref, data_ref,
    out_ref, npot_ref, dpot_ref,
    stage, nbuf, dbuf, pbuf, abuf, bbuf, rbuf, cbuf, gbuf, gall, ubuf, labuf,
    massbuf, plow, tbuf, vbuf,
    ns, nr, ds_, dr, sib_s, sib_r, as_, ar, bs, br, cs, cr, gs, gr, os_, or_,
):
    FQ = width // (Q * C)
    half = C // 2
    eps = 1.0 / math.sqrt(width)
    row = lax.axis_index("row")
    c = lax.axis_index("col")
    q = row // 2
    k = row % 2
    other = 1 - k
    sibling = (q * 2 + other, c)

    def data_target(j):
        chunk = row * half + j
        return (chunk % Q) * 2 + c // half, chunk // Q

    source_row = (c * Q + q) // half

    def data_source(j):
        return source_row, k * half + j

    to_self = jnp.logical_and(source_row == row, c // half == k)
    n_self = jnp.where(to_self, 1, 0).astype(jnp.int32)

    barrier = pltpu.get_barrier_semaphore()

    def greet(device):
        pl.semaphore_signal(barrier, inc=1, device_id=device, device_id_type=MESH)

    def greet_row(s, carry):
        greet((lax.rem(q + s, Q) * 2 + k, c))
        return carry

    def greet_col(s, carry):
        greet((row, lax.rem(c + s, C)))
        return carry

    def greet_source(j, carry):
        sr, sc = data_source(j)

        @pl.when(jnp.logical_or(sr != row, sc != c))
        def _():
            greet((sr, sc))

        return carry

    greet(sibling)
    lax.fori_loop(1, Q, greet_row, 0)
    lax.fori_loop(0, half, greet_source, 0)
    lax.fori_loop(1, C, greet_col, 0)

    rows8 = lax.broadcasted_iota(jnp.int32, (8, LANES), 0)
    lanes1 = lax.broadcasted_iota(jnp.int32, (1, LANES), 1)
    own_w = jnp.zeros((8, LANES), jnp.int32)
    for i in range(8):
        own_w = jnp.where(rows8 == i, nw_ref[i], own_w)
    own_w = own_w.astype(F32).astype(BF16)
    for j in range(Q):
        stage[j, :, 0:FQ] = noise_ref[:, j * FQ:(j + 1) * FQ]
        stage[j, :, FQ:FQ + LANES] = own_w

    data_w = jnp.zeros((1, LANES), jnp.int32)
    base = (c % 4) * 32
    for i in range(32):
        data_w = jnp.where(lanes1 == base + i, dw_ref[i], data_w)
    cbuf[...] = jnp.zeros_like(cbuf)
    cbuf[2:3, :] = data_w.astype(F32)

    pl.semaphore_wait(barrier, (Q - 1) + (C - 1) + 1 + half - n_self)

    def send_data(j, carry):
        tr, tc = data_target(j)
        src = data_ref.at[:, pl.ds(pl.multiple_of(j * FQ, FQ), FQ)]
        is_self = jnp.logical_and(tr == row, tc == c)

        @pl.when(is_self)
        def _():
            pltpu.make_async_copy(src, dbuf.at[c], dr).start()

        @pl.when(jnp.logical_not(is_self))
        def _():
            pltpu.make_async_remote_copy(
                src, dbuf.at[c], ds_, dr, device_id=(tr, tc), device_id_type=MESH
            ).start()

        return carry

    lax.fori_loop(0, half, send_data, 0)

    def send_noise(s, carry):
        t = lax.rem(q + s, Q)
        pltpu.make_async_remote_copy(
            stage.at[t], nbuf.at[k, q], ns, nr,
            device_id=(t * 2 + k, c), device_id_type=MESH,
        ).start()
        return carry

    lax.fori_loop(1, Q, send_noise, 0)
    pltpu.make_async_copy(stage.at[q], nbuf.at[k, q], nr).start()
    pltpu.make_async_copy(nbuf.at[k], nbuf.at[k], nr).wait()

    noise_swap = pltpu.make_async_remote_copy(
        nbuf.at[k], nbuf.at[k], sib_s.at[0], sib_r.at[0],
        device_id=sibling, device_id_type=MESH,
    )
    noise_swap.start()

    own_data = dbuf.at[pl.ds(k * half, half)]
    pltpu.make_async_copy(own_data, own_data, dr).wait()
    data_swap = pltpu.make_async_remote_copy(
        own_data, own_data, sib_s.at[1], sib_r.at[1],
        device_id=sibling, device_id_type=MESH,
    )
    data_swap.start()
    dblock = dbuf[pl.ds(k * half, half)].reshape(half * 32, FQ)
    df = dblock.astype(F32)
    d2 = df * df
    d2_hi = d2.astype(BF16)
    d2_lo = (d2 - d2_hi.astype(F32)).astype(BF16)
    ones = jnp.ones((8, FQ), BF16)
    nt = (((1,), (1,)), ((), ()))
    dsq = lax.dot_general(ones, d2_hi, nt, preferred_element_type=F32)
    dsq = dsq + lax.dot_general(ones, d2_lo, nt, preferred_element_type=F32)
    dsq = dsq[0:1, :]

    pltpu.make_async_copy(nbuf.at[other], nbuf.at[other], sib_r.at[0]).wait()
    nf = nbuf[:, :, :, 0:FQ].astype(F32).reshape(16 * Q, FQ)
    wa = nbuf[:, :, :, FQ:FQ + LANES].astype(F32).reshape(16 * Q, LANES)
    nsq = jnp.sum(nf * nf, axis=1, keepdims=True)
    cross = lax.dot_general(nf.astype(BF16), dblock, nt, preferred_element_type=F32)
    part = nsq + dsq - 2.0 * cross
    for h in range(2):
        pbuf[:, h] = part[:, h * LANES:(h + 1) * LANES].reshape(Q, 16, LANES)

    def send_a(s, carry):
        t = lax.rem(q + s, Q)
        pltpu.make_async_remote_copy(
            pbuf.at[t], abuf.at[q], as_, ar,
            device_id=(t * 2 + k, c), device_id_type=MESH,
        ).start()
        return carry

    lax.fori_loop(1, Q, send_a, 0)
    pltpu.make_async_copy(pbuf.at[q], abuf.at[q], ar).start()
    w_sum = jnp.sum(wa, axis=0, keepdims=True)
    labuf[...] = jnp.log(wa / w_sum).reshape(Q, 16, LANES)
    pltpu.make_async_copy(abuf, abuf, ar).wait()
    total = abuf[0]
    for j in range(1, Q):
        total = total + abuf[j]

    for i in range(C):
        h, t = i // 8, i % 8
        bbuf[i] = total[h, 2 * t:2 * t + 2, :]

    def send_b(s, carry):
        t = lax.rem(c + s, C)
        pltpu.make_async_remote_copy(
            bbuf.at[t], rbuf.at[c], bs, br,
            device_id=(row, t), device_id_type=MESH,
        ).start()
        return carry

    lax.fori_loop(1, C, send_b, 0)
    pltpu.make_async_copy(bbuf.at[c], rbuf.at[c], br).start()
    pltpu.make_async_copy(rbuf, rbuf, br).wait()
    cbuf[0:2, :] = jnp.sum(rbuf[...], axis=0)

    def send_c(s, carry):
        t = lax.rem(c + s, C)
        pltpu.make_async_remote_copy(
            cbuf, gbuf.at[c], cs, cr, device_id=(row, t), device_id_type=MESH,
        ).start()
        return carry

    lax.fori_loop(1, C, send_c, 0)
    pltpu.make_async_copy(cbuf, gbuf.at[c], cr).start()
    pltpu.make_async_copy(gbuf, gbuf, cr).wait()
    for i in range(C):
        h, t = i // 8, i % 8
        gall[k, q, h, 2 * t:2 * t + 2, :] = gbuf[i, 0:2, :]

    def send_g(s, carry):
        t = lax.rem(q + s, Q)
        pltpu.make_async_remote_copy(
            gall.at[k, q], gall.at[k, q], gs, gr,
            device_id=(t * 2 + k, c), device_id_type=MESH,
        ).start()
        return carry

    lax.fori_loop(1, Q, send_g, 0)
    dw = [
        sum(gbuf[i, 2:3, :] for i in range(4 * b + 1, 4 * b + 4)) + gbuf[4 * b, 2:3, :]
        for b in range(C // 4)
    ]
    dw = jnp.concatenate(dw, axis=0)
    dw_sum = jnp.sum(jnp.sum(dw, axis=0, keepdims=True), axis=1, keepdims=True)
    log_b = jnp.log(dw / dw_sum).reshape(2, 2, 1, LANES)

    others = gall.at[k, pl.ds(0, Q - 1)]
    pltpu.make_async_copy(others, others, gr).wait()
    cost_swap = pltpu.make_async_remote_copy(
        gall.at[k], gall.at[k], sib_s.at[2], sib_r.at[2],
        device_id=sibling, device_id_type=MESH,
    )
    cost_swap.start()
    pltpu.make_async_copy(gall.at[other], gall.at[other], sib_r.at[2]).wait()

    scale = -1.0 / (width * eps)

    def scores(j):
        return gall[:, j] * scale

    v = jnp.zeros((2, 2, 1, LANES), F32)
    for rounds in range(HALVES // 2):

        def row_step(j, peak):
            s = scores(j)
            z = s + v
            m = jnp.max(jnp.max(z, axis=(0, 1)), axis=1, keepdims=True)
            e = jnp.sum(jnp.sum(jnp.exp(z - m), axis=(0, 1)), axis=1, keepdims=True)
            u = labuf[j] - (m + jnp.log(e))
            ubuf[j] = u
            return jnp.maximum(peak, jnp.max(s + u, axis=2, keepdims=True))

        peak = lax.fori_loop(
            0, Q, row_step, jnp.full((2, 2, 1, LANES), -jnp.inf, F32)
        )

        def col_step(j, acc):
            return acc + jnp.exp(scores(j) + ubuf[j] - peak)

        acc = lax.fori_loop(0, Q, col_step, jnp.zeros((2, 2, 16, LANES), F32))
        v = log_b - (peak + jnp.log(jnp.sum(acc, axis=2, keepdims=True)))

    def plan_step(j, carry):
        own = k * (Q // 2) + j
        p = jnp.exp(ubuf[own] + v + scores(own))
        massbuf[j] = jnp.broadcast_to(
            jnp.sum(jnp.sum(p, axis=(0, 1)), axis=1, keepdims=True), (16, LANES)
        )
        for b in range(4):
            plow[j, :, b * LANES:(b + 1) * LANES] = p[b // 2, b % 2].astype(BF16)
        return carry

    lax.fori_loop(0, Q // 2, plan_step, 0)

    pltpu.make_async_copy(
        dbuf.at[pl.ds(other * half, half)], dbuf.at[pl.ds(other * half, half)], sib_r.at[1]
    ).wait()
    value = jnp.dot(
        plow[...].reshape(8 * Q, C * 32), dbuf[...].reshape(C * 32, FQ),
        preferred_element_type=F32,
    )
    mass = massbuf[...].reshape(8 * Q, LANES)
    value = value / jnp.concatenate([mass] * (FQ // LANES), axis=1)
    tbuf[...] = value.reshape(Q, 8, FQ).astype(BF16)

    def send_t(s, carry):
        t = lax.rem(q + s, Q)
        pltpu.make_async_remote_copy(
            tbuf.at[t], out_ref.at[q], os_, or_,
            device_id=(t * 2 + k, c), device_id_type=MESH,
        ).start()
        return carry

    lax.fori_loop(1, Q, send_t, 0)
    pltpu.make_async_copy(tbuf.at[q], out_ref.at[q], or_).start()

    pair = ubuf[k * (Q // 2) + q // 2]
    own_u = jnp.where(q % 2 == 0, pair[0:8], pair[8:16])
    lanes8 = lax.broadcasted_iota(jnp.int32, (8, LANES), 1)
    own_u = jnp.sum(jnp.where(rows8 == lanes8, own_u, 0.0), axis=0, keepdims=True)
    npot_ref[...] = own_u[:, 0:8] * eps
    for b in range(4):
        vbuf[b] = v[b // 2, b % 2]
    block = vbuf[c // 4]
    own_v = block[:, 0:32]
    for t in range(1, 4):
        own_v = jnp.where(c % 4 == t, block[:, 32 * t:32 * t + 32], own_v)
    dpot_ref[...] = own_v * eps

    def sent(ref, sem):
        pltpu.make_async_copy(ref, ref, sem).wait()

    sent(stage.at[pl.ds(0, Q - 1)], ns)

    @pl.when(to_self)
    def _():
        sent(dbuf.at[pl.ds(0, half - 1)], ds_)

    @pl.when(jnp.logical_not(to_self))
    def _():
        sent(dbuf.at[pl.ds(0, half)], ds_)

    noise_swap.wait_send()
    data_swap.wait_send()
    cost_swap.wait_send()
    sent(pbuf.at[pl.ds(0, Q - 1)], as_)
    sent(bbuf.at[pl.ds(0, C - 1)], bs)
    sent(gbuf.at[pl.ds(0, C - 1)], cs)
    sent(others, gs)
    sent(tbuf.at[pl.ds(0, Q - 1)], os_)
    sent(out_ref, or_)


def per_device(Q, C, noise, data, noise_weight, data_weight):
    width = noise.shape[1] * C
    FQ = width // (Q * C)
    vmem = pl.BlockSpec(memory_space=pltpu.VMEM)
    smem = pl.BlockSpec(memory_space=pltpu.SMEM)
    anywhere = pl.BlockSpec(memory_space=pl.ANY)
    targets, noise_pot, data_pot = pl.pallas_call(
        functools.partial(kernel, Q, C, width),
        out_shape=(
            jax.ShapeDtypeStruct((Q, 8, FQ), BF16),
            jax.ShapeDtypeStruct((1, 8), F32),
            jax.ShapeDtypeStruct((1, 32), F32),
        ),
        in_specs=[smem, smem, vmem, anywhere],
        out_specs=(anywhere, vmem, vmem),
        scratch_shapes=[
            pltpu.VMEM((Q, 8, FQ + LANES), BF16),
            pltpu.VMEM((2, Q, 8, FQ + LANES), BF16),
            pltpu.VMEM((C, 32, FQ), BF16),
            pltpu.VMEM((Q, 2, 16, LANES), F32),
            pltpu.VMEM((Q, 2, 16, LANES), F32),
            pltpu.VMEM((C, 2, LANES), F32),
            pltpu.VMEM((C, 2, LANES), F32),
            pltpu.VMEM((4, LANES), F32),
            pltpu.VMEM((C, 4, LANES), F32),
            pltpu.VMEM((2, Q, 2, 16, LANES), F32),
            pltpu.VMEM((Q, 16, LANES), F32),
            pltpu.VMEM((Q, 16, LANES), F32),
            pltpu.VMEM((Q // 2, 16, LANES), F32),
            pltpu.VMEM((Q // 2, 16, C * 32), BF16),
            pltpu.VMEM((Q, 8, FQ), BF16),
            pltpu.VMEM((4, 1, LANES), F32),
        ] + [pltpu.SemaphoreType.DMA] * 4
        + [pltpu.SemaphoreType.DMA((3,))] * 2
        + [pltpu.SemaphoreType.DMA] * 10,
        compiler_params=pltpu.CompilerParams(
            collective_id=0, has_side_effects=True, vmem_limit_bytes=32 * 1024 * 1024
        ),
    )(noise_weight, data_weight, noise, data)
    targets = jnp.transpose(targets, (1, 0, 2)).reshape(8, Q * FQ)
    return (targets, noise_pot.reshape(8), data_pot.reshape(32))


def solution(mesh):
    placed = (P("row", "col"), P("col", "row"), P("row"), P("col"))
    return jax.shard_map(
        functools.partial(per_device, mesh.shape["row"] // 2, mesh.shape["col"]),
        mesh=mesh,
        in_specs=placed,
        out_specs=(P("row", "col"), P("row"), P("col")),
        check_vma=False,
    )
```

time: 944 us -> 77.9 us (0.08)
  blocking collectives: 582 us -> 0 us
  waiting for transfers between devices: 326 us -> 0 us
  Pallas kernels: 0 us -> 72.3 us
  between operations: 13.8 us -> 0.65 us
  other arithmetic: 11.6 us -> 0 us
    psum x6 -> x0, blocking collectives: 334 us -> none  [the longest x2 135 us: lse_over_noise(): total = lax.psum(jnp.sum(jnp.exp(scores - peak[None, :]), axis=0), 'row')]
    pmax x4 -> x0, blocking collectives: 248 us -> none  [the longest x2 156 us: lse_over_noise(): peak = lax.pmax(local_peak, 'row')]
    reduce_scatter x1 -> x0, waiting for transfers between devices: 167 us -> none  [per_device(): lax.psum_scatter(partial_value.astype(jnp.bfloat16), 'col', scatter_dimen...]
    all_gather x2 -> x0, waiting for transfers between devices: 158 us -> none  [the longest x1 90.7 us: per_device(): noise_full = lax.all_gather(noise, 'col', axis=1, tiled=True)]
    pallas_call x0 -> x1, Pallas kernels: none -> 72.3 us  [per_device(): pl.pallas_call(functools.partial(kernel, Q, C, width), out_shape=(jax.Sha...]
  transfers between devices with their start and end apart: 3 -> 0, of which waited for: 3 -> 0; matrix products, arithmetic and copies ran while one was open for 0% -> 0% of each run, Pallas kernels for 0% -> 0%
where the time goes in v1:
time: 77.9 us; the launch traced here: 77.7 us
  Pallas kernels  72.3 us (93%)
  local copies, waits for them, and re-layouts  4.7 us (6%)
    pallas_call x1, Pallas kernels, per_device(): pl.pallas_call(functools.partial(kernel, Q, C, width), out_shape=(jax.Sha...  72.3 us
    unnamed x11, local copies, waits for them, and re-layouts  4.7 us

profile of v1, /device:TPU:1, one launch (start us, length us, event | category | flops | bytes accessed | tf_op | source)
XLA Modules:
  0.0 77.7 jit_solution(1536287046764500661)
XLA Ops:
  0.6 0.0 copy-start
  0.6 0.9 %copy-done = bf16[32,2048]{1,0:T(8,128)(2,1)S(1)} copy-done((bf16[32,2048]{1,0:T(8,128)(2,1)S(1)}, bf16[32,2048]{1,0:T(8,128)(2,1)}, u32[]{:S(2)}) %copy-start) | copy-done | bytes 131096
  1.5 0.0 copy-start.1
  1.5 0.8 %copy-done.1 = bf16[8,4096]{1,0:T(8,128)(2,1)S(1)} copy-done((bf16[8,4096]{1,0:T(8,128)(2,1)S(1)}, bf16[8,4096]{1,0:T(8,128)(2,1)}, u32[]{:S(2)}) %copy-start.1) | copy-done | bytes 65560
  2.4 0.0 copy-start.2
  2.4 0.7 copy-done.2
  3.0 0.0 copy-start.3
  3.0 0.7 copy-done.3
  3.7 72.3 %shard_map.67 = (bf16[16,8,256]{2,1,0:T(8,128)(2,1)S(1)}, f32[1,8]{1,0:T(1,128)S(1)}, f32[1,32]{1,0:T(1,128)S(1)}) custom-call(s32[8]{0:T(128)S(1)} %copy-done.2, s32[32]{0:T(128)S(1)} %copy-done.3, bf16[8,4096]{1,0:T(8,128)(2,1)S(1)} %copy-done.1, bf16[32,2048]{1,0:T(8,128)(2,1)S(1)} %copy-done), custom_call_target="tpu_custom_call" | custom-call | tf_op jit(solution)/shard_map/pallas_call | solution.py:336
  76.0 0.6 copy.10
  76.7 0.5 copy.11
  77.2 0.5 copy.12
Async XLA Ops:
  0.6 0.9 %copy-start = (bf16[32,2048]{1,0:T(8,128)(2,1)S(1)}, bf16[32,2048]{1,0:T(8,128)(2,1)}, u32[]{:S(2)}) copy-start(bf16[32,2048]{1,0:T(8,128)(2,1)} %data_ref.1) | copy-start | bytes 393220
  1.5 0.8 %copy-start.1 = (bf16[8,4096]{1,0:T(8,128)(2,1)S(1)}, bf16[8,4096]{1,0:T(8,128)(2,1)}, u32[]{:S(2)}) copy-start(bf16[8,4096]{1,0:T(8,128)(2,1)} %noise_ref.1) | copy-start | bytes 196612
  2.4 0.7 copy-start.2
  3.0 0.7 copy-start.3

commit v2 on v0

v2 whole, which is shorter than its diff:
```python
import functools
import math

import jax
import jax.numpy as jnp
from jax import lax
from jax.experimental import pallas as pl
from jax.experimental.pallas import tpu as pltpu
from jax.sharding import PartitionSpec as P

HALVES = 4
MESH = pl.DeviceIdType.MESH
F32 = jnp.float32
BF16 = jnp.bfloat16
LANES = 128
X, YL, Z, YH = 4, 4, 8, 2
Y = YH * YL
Q = YL * X
C = Z * YH
NT = (((1,), (1,)), ((), ()))


def kernel(
    width,
    nw_hbm, dw_hbm, noise_ref, data_ref,
    out_ref, npot_ref, dpot_ref,
    nw_ref, dw_ref, nstage, dvm, dstage, wstage, nbuf, nmat, dcrit, dbuf, wbuf,
    pbuf, abuf, bbuf, rbuf, gall, lbuf, vbuf, plan, tbuf,
    load, ns, nr, cs, cr, ts, tr, ws, wr, sib_s, sib_r, as_, ar, bs, br,
    gs, gr, hs, hr, os_, or_,
):
    FQ = width // (Q * C)
    FS = X * FQ
    half = C // 2
    eps = 1.0 / math.sqrt(width)
    row = lax.axis_index("row")
    c = lax.axis_index("col")
    k = row % 2
    q = row // 2
    x = q % X
    yl = q // X
    z = c // YH
    yh = c % YH
    y = yh * YL + yl
    other = 1 - k

    def place(yl_, x_, k_):
        return (yl_ * X + x_) * 2 + k_

    sibling = (place(yl, x, other), c)

    def data_target(j):
        return (k * half + j) * 2 + c // half, q

    source_row = c * 2 + yl // 2
    to_self = jnp.logical_and(source_row == row, c // half == k)
    n_self = jnp.where(to_self, 1, 0).astype(jnp.int32)

    def finish():
        def sent(ref, sem):
            pltpu.make_async_copy(ref, ref, sem).wait()

        def sent_targets(ref, sem):
            @pl.when(to_self)
            def _():
                sent(ref.at[pl.ds(0, half - 1)], sem)

            @pl.when(jnp.logical_not(to_self))
            def _():
                sent(ref.at[pl.ds(0, half)], sem)

        sent_targets(dstage, cs)
        sent_targets(dbuf, ts)
        sent_targets(wbuf, ws)
        sent(nbuf.at[k, pl.ds(0, Q - 1)], ns)
        sent(nbuf.at[k], sib_s.at[0])
        sent(pbuf.at[pl.ds(0, Y - 1)], as_)
        sent(rbuf.at[pl.ds(0, Z - 1)], bs)
        sent(dbuf.at[pl.ds(0, half)], sib_s.at[1])
        sent(wbuf.at[pl.ds(0, half)], sib_s.at[2])
        sent(gall.at[k, x, pl.ds(0, Y - 1)], gs)
        sent(gall.at[k, pl.ds(0, X - 1)], hs)
        sent(gall.at[k], sib_s.at[3])
        sent(tbuf.at[pl.ds(0, Q - 1)], os_)
        sent(out_ref, or_)

    loads = [
        pltpu.make_async_copy(nw_hbm, nw_ref, load.at[0]),
        pltpu.make_async_copy(dw_hbm, dw_ref, load.at[1]),
        pltpu.make_async_copy(data_ref, dvm, load.at[2]),
    ] + [
        pltpu.make_async_copy(
            noise_ref.at[:, pl.ds(t * FS, FS)], nstage.at[t, :, pl.ds(0, FS)], load.at[3 + t]
        )
        for t in range(YL)
    ]

    barrier = pltpu.get_barrier_semaphore()

    def greet(device):
        pl.semaphore_signal(barrier, inc=1, device_id=device, device_id_type=MESH)

    def greet_source(j, carry):
        sc = k * half + j

        @pl.when(jnp.logical_or(source_row != row, sc != c))
        def _():
            greet((source_row, sc))

        return carry

    def greet_z(s, carry):
        greet((row, lax.rem(z + s, Z) * YH + yh))
        return carry

    def greet_y(t, carry):
        greet((place(t, x, k), z * YH + 1 - yh))
        return carry

    def greet_row(s, carry):
        greet((lax.rem(q + s, Q) * 2 + k, c))
        return carry

    lax.fori_loop(0, half, greet_source, 0)
    lax.fori_loop(1, Z, greet_z, 0)
    lax.fori_loop(0, YL, greet_y, 0)
    lax.fori_loop(1, Q, greet_row, 0)
    greet(sibling)
    for copy in loads:
        copy.start()

    for copy in loads:
        copy.wait()

    for j in range(2 * X):
        s, t = j // X, j % X
        dstage[j] = jnp.concatenate(
            [
                dvm[:, s * FS + f * FQ:s * FS + (f + 1) * FQ].astype(F32)[8 * t:8 * t + 8]
                for f in range(X)
            ],
            axis=0,
        ).astype(BF16)
    rows32 = lax.broadcasted_iota(jnp.int32, (32, LANES), 0)
    data_w = jnp.zeros((32, LANES), jnp.int32)
    for i in range(32):
        data_w = jnp.where(rows32 == i, dw_ref[i], data_w)
    wstage[...] = data_w.astype(F32).astype(BF16)

    rows8 = lax.broadcasted_iota(jnp.int32, (8, LANES), 0)
    lanes8 = lax.broadcasted_iota(jnp.int32, (8, LANES), 1)
    noise_w = jnp.zeros((8, LANES), jnp.int32)
    for i in range(8):
        noise_w = jnp.where(rows8 == i, nw_ref[i], noise_w)
    noise_w = noise_w.astype(F32)
    for t in range(YL):
        nf = nstage[t, :, 0:FS].astype(F32)
        sq = jnp.sum(nf * nf, axis=1, keepdims=True)
        hi = sq.astype(BF16).astype(F32)
        mid = (sq - hi).astype(BF16).astype(F32)
        lo = sq - hi - mid
        tail = jnp.where(lanes8 == 3, noise_w, 0.0)
        tail = jnp.where(lanes8 == 2, lo, tail)
        tail = jnp.where(lanes8 == 1, mid, tail)
        tail = jnp.where(lanes8 == 0, hi, tail)
        nstage[t, :, FS:FS + LANES] = tail.astype(BF16)

    pl.semaphore_wait(barrier, (Q - 1) + (Z - 1) + YL + 1 + half - n_self)

    def to_targets(src_of, dst, send, recv):
        def step(j, carry):
            device = data_target(j)
            is_self = jnp.logical_and(device[0] == row, device[1] == c)

            @pl.when(is_self)
            def _():
                pltpu.make_async_copy(src_of(j), dst, recv).start()

            @pl.when(jnp.logical_not(is_self))
            def _():
                pltpu.make_async_remote_copy(
                    src_of(j), dst, send, recv, device_id=device, device_id_type=MESH
                ).start()

            return carry

        lax.fori_loop(0, half, step, 0)

    to_targets(lambda j: dstage.at[j], dcrit.at[c % half], cs, cr)

    def send_noise(s, carry):
        t = lax.rem(q + s, Q)
        pltpu.make_async_remote_copy(
            nstage.at[t // X], nbuf.at[k, q], ns, nr,
            device_id=(t * 2 + k, c), device_id_type=MESH,
        ).start()
        return carry

    lax.fori_loop(1, Q, send_noise, 0)
    pltpu.make_async_copy(nstage.at[yl], nbuf.at[k, q], nr).start()

    to_targets(
        lambda j: data_ref.at[:, pl.ds(pl.multiple_of(j * FQ, FQ), FQ)], dbuf.at[c], ts, tr
    )
    to_targets(lambda j: wstage, wbuf.at[c], ws, wr)

    def arrived(ref, sem):
        pltpu.make_async_copy(ref, ref, sem).wait()

    def swap(ref, i):
        return pltpu.make_async_remote_copy(
            ref, ref, sib_s.at[i], sib_r.at[i], device_id=sibling, device_id_type=MESH
        )

    def noise_rows(core):
        for t in range(2):
            part = nbuf[core, t * (Q // 2):(t + 1) * (Q // 2)].astype(F32)
            nmat[core, t * 4 * Q:(t + 1) * 4 * Q, :] = part.reshape(4 * Q, FS + LANES).astype(BF16)

    arrived(nbuf.at[k], nr)
    noise_swap = swap(nbuf.at[k], 0)
    noise_swap.start()
    noise_rows(k)
    arrived(nbuf.at[other], sib_r.at[0])
    noise_rows(other)
    tail = nmat[:, :, FS:FS + LANES].reshape(16 * Q, LANES)
    pick_sq = jnp.where(lanes8 < 3, 1.0, 0.0).astype(BF16)
    pick_w = jnp.where(lanes8 == 3, 1.0, 0.0).astype(BF16)
    nsq = lax.dot_general(pick_sq, tail, NT, preferred_element_type=F32)[0:1, :]
    wa = lax.dot_general(pick_w, tail, NT, preferred_element_type=F32)[0:1, :]

    arrived(dcrit, cr)
    df = dcrit[...].astype(F32).reshape(half, X, 8, FQ)
    part = jnp.sum(
        jnp.sum(df * df, axis=1).reshape(half * 8, FQ), axis=1, keepdims=True
    ) + nsq
    dm = (df * -2.0)
    for f in range(X):
        part = part + lax.dot_general(
            dm[:, f].reshape(half * 8, FQ).astype(BF16),
            nmat[:, :, f * FQ:(f + 1) * FQ].reshape(16 * Q, FQ),
            NT, preferred_element_type=F32,
        )
    for h in range(2):
        pbuf[:, h] = part[:, h * LANES:(h + 1) * LANES].reshape(Y, 8, LANES)

    def y_peer(t):
        return place(t % YL, x, k), z * YH + t // YL

    def send_a(s, carry):
        t = lax.rem(y + s, Y)
        pltpu.make_async_remote_copy(
            pbuf.at[t], abuf.at[y], as_, ar, device_id=y_peer(t), device_id_type=MESH
        ).start()
        return carry

    lax.fori_loop(1, Y, send_a, 0)
    pltpu.make_async_copy(pbuf.at[y], abuf.at[y], ar).start()
    log_a = jnp.log(wa / jnp.sum(wa, axis=1, keepdims=True))
    log_a = [log_a[:, h * LANES:(h + 1) * LANES] for h in range(2)]
    arrived(abuf, ar)
    total = abuf[0]
    for j in range(1, Y):
        total = total + abuf[j]
    bbuf[...] = total

    def send_b(s, carry):
        t = lax.rem(z + s, Z)
        pltpu.make_async_remote_copy(
            bbuf, rbuf.at[z], bs, br, device_id=(row, t * YH + yh), device_id_type=MESH
        ).start()
        return carry

    lax.fori_loop(1, Z, send_b, 0)
    pltpu.make_async_copy(bbuf, rbuf.at[z], br).start()

    own_data = dbuf.at[pl.ds(k * half, half)]
    arrived(own_data, tr)
    data_swap = swap(own_data, 1)
    data_swap.start()
    own_w = wbuf.at[pl.ds(k * half, half)]
    arrived(own_w, wr)
    w_swap = swap(own_w, 2)
    w_swap.start()

    arrived(rbuf, br)
    total = rbuf[0]
    for j in range(1, Z):
        total = total + rbuf[j]
    gall[k, x, y] = total * (-1.0 / (width * eps))

    def send_g(s, carry):
        t = lax.rem(y + s, Y)
        pltpu.make_async_remote_copy(
            gall.at[k, x, y], gall.at[k, x, y], gs, gr,
            device_id=y_peer(t), device_id_type=MESH,
        ).start()
        return carry

    lax.fori_loop(1, Y, send_g, 0)

    arrived(wbuf.at[pl.ds(other * half, half)], sib_r.at[2])
    wb = wbuf[...].astype(F32)
    w_sum = jnp.sum(jnp.sum(wb, axis=0), axis=0, keepdims=True)
    log_b = jnp.log(wb / w_sum).reshape(2, half, X, 8, LANES)
    for t in range(X):
        lbuf[:, t] = log_b[:, :, t]

    arrived(gall.at[k, x, pl.ds(0, Y - 1)], gr)

    def send_h(s, carry):
        t = lax.rem(x + s, X)
        pltpu.make_async_remote_copy(
            gall.at[k, x], gall.at[k, x], hs, hr,
            device_id=(place(yl, t, k), c), device_id_type=MESH,
        ).start()
        return carry

    lax.fori_loop(1, X, send_h, 0)
    arrived(gall.at[k, pl.ds(0, X - 1)], hr)
    cost_swap = swap(gall.at[k], 3)
    cost_swap.start()
    arrived(gall.at[other], sib_r.at[3])

    def parts(i):
        return i // X, i % X

    def peak_step(i, peak):
        a, b = parts(i)
        return jnp.maximum(peak, jnp.max(gall[a, b], axis=0))

    peak = lax.fori_loop(0, 2 * X, peak_step, jnp.full((2, 8, LANES), -jnp.inf, F32))
    for rounds in range(HALVES // 2):
        top = jnp.max(peak, axis=1, keepdims=True)

        def noise_step(i, acc):
            a, b = parts(i)
            s = gall[a, b]
            if rounds:
                s = s + vbuf[a, b][:, None]
            return acc + jnp.sum(jnp.exp(s - top), axis=0)

        acc = lax.fori_loop(0, 2 * X, noise_step, jnp.zeros((2, 8, LANES), F32))
        lse = top + jnp.log(jnp.sum(acc, axis=1, keepdims=True))
        u = jnp.concatenate([(log_a[h] - lse[h])[None] for h in range(2)], axis=0)

        def data_step(i, peak):
            a, b = parts(i)
            s = gall[a, b]
            w = s + u
            m = jnp.max(jnp.max(w, axis=1), axis=2, keepdims=True)
            e = jnp.sum(jnp.sum(jnp.exp(w - m[:, None]), axis=1), axis=2, keepdims=True)
            v = lbuf[a, b] - (m + jnp.log(e))
            vbuf[a, b] = v
            return jnp.maximum(peak, jnp.max(s + v[:, None], axis=0))

        peak = lax.fori_loop(0, 2 * X, data_step, jnp.full((2, 8, LANES), -jnp.inf, F32))

    own_u = jnp.where(k == 0, u[0], u[1])
    for i in range(2 * X):
        a, b = parts(i)
        plan[a, :, b] = jnp.exp(gall[a, b, :, k] + own_u + vbuf[a, b])
    p = jnp.transpose(plan[...].reshape(C * 32, LANES), (1, 0))
    mass = jnp.sum(p, axis=1, keepdims=True)

    arrived(dbuf.at[pl.ds(other * half, half)], sib_r.at[1])
    value = jnp.dot(
        p.astype(BF16), dbuf[...].reshape(C * 32, FQ), preferred_element_type=F32
    ) / mass
    tbuf[...] = value.reshape(Q, 8, FQ).astype(BF16)

    def send_t(s, carry):
        t = lax.rem(q + s, Q)
        pltpu.make_async_remote_copy(
            tbuf.at[t], out_ref.at[q], os_, or_,
            device_id=(t * 2 + k, c), device_id_type=MESH,
        ).start()
        return carry

    lax.fori_loop(1, Q, send_t, 0)
    pltpu.make_async_copy(tbuf.at[q], out_ref.at[q], or_).start()

    mine = own_u[:, 0:8]
    for t in range(1, Q):
        mine = jnp.where(q == t, own_u[:, 8 * t:8 * t + 8], mine)
    npot_ref[...] = mine * eps
    lanes4 = lax.broadcasted_iota(jnp.int32, (X, 8, LANES), 2)
    index4 = lax.broadcasted_iota(jnp.int32, (X, 8, LANES), 0) * 8 + lax.broadcasted_iota(
        jnp.int32, (X, 8, LANES), 1
    )
    block = jnp.where(lanes4 == index4, vbuf[c // half, :, c % half], 0.0)
    block = jnp.sum(jnp.sum(block, axis=0), axis=0, keepdims=True)
    dpot_ref[...] = block[:, 0:32] * eps
    finish()


def per_device(noise, data, noise_weight, data_weight):
    width = noise.shape[1] * C
    FQ = width // (Q * C)
    FS = X * FQ
    vmem = pl.BlockSpec(memory_space=pltpu.VMEM)
    anywhere = pl.BlockSpec(memory_space=pl.ANY)
    dma = pltpu.SemaphoreType.DMA
    targets, noise_pot, data_pot = pl.pallas_call(
        functools.partial(kernel, width),
        out_shape=(
            jax.ShapeDtypeStruct((Q, 8, FQ), BF16),
            jax.ShapeDtypeStruct((1, 8), F32),
            jax.ShapeDtypeStruct((1, 32), F32),
        ),
        in_specs=[anywhere] * 4,
        out_specs=(anywhere, vmem, vmem),
        scratch_shapes=[
            pltpu.SMEM((8,), jnp.int32),
            pltpu.SMEM((32,), jnp.int32),
            pltpu.VMEM((YL, 8, FS + LANES), BF16),
            pltpu.VMEM((32, 2 * FS), BF16),
            pltpu.VMEM((2 * X, 32, FQ), BF16),
            pltpu.VMEM((32, LANES), BF16),
            pltpu.VMEM((2, Q, 8, FS + LANES), BF16),
            pltpu.VMEM((2, 8 * Q, FS + LANES), BF16),
            pltpu.VMEM((C // 2, 32, FQ), BF16),
            pltpu.VMEM((C, 32, FQ), BF16),
            pltpu.VMEM((C, 32, LANES), BF16),
            pltpu.VMEM((Y, 2, 8, LANES), F32),
            pltpu.VMEM((Y, 2, 8, LANES), F32),
            pltpu.VMEM((2, 8, LANES), F32),
            pltpu.VMEM((Z, 2, 8, LANES), F32),
            pltpu.VMEM((2, X, Y, 2, 8, LANES), F32),
            pltpu.VMEM((2, X, Y, 8, LANES), F32),
            pltpu.VMEM((2, X, Y, 8, LANES), F32),
            pltpu.VMEM((2, Y, X, 8, LANES), F32),
            pltpu.VMEM((Q, 8, FQ), BF16),
            dma((3 + YL,)),
        ] + [dma] * 8 + [dma((4,))] * 2 + [dma] * 10,
        compiler_params=pltpu.CompilerParams(
            collective_id=0, has_side_effects=True, vmem_limit_bytes=60 * 1024 * 1024
        ),
    )(noise_weight, data_weight, noise, data)
    targets = jnp.transpose(targets, (1, 0, 2)).reshape(8, Q * FQ)
    return (targets, noise_pot.reshape(8), data_pot.reshape(32))


def solution(mesh):
    placed = (P("row", "col"), P("col", "row"), P("row"), P("col"))
    return jax.shard_map(
        per_device,
        mesh=mesh,
        in_specs=placed,
        out_specs=(P("row", "col"), P("row"), P("col")),
        check_vma=False,
    )
```

time: 944 us -> 73 us (0.08)
  blocking collectives: 582 us -> 0 us
  waiting for transfers between devices: 326 us -> 0 us
  Pallas kernels: 0 us -> 69 us
  between operations: 13.8 us -> 0.65 us
  other arithmetic: 11.6 us -> 0 us
    psum x6 -> x0, blocking collectives: 334 us -> none  [the longest x2 135 us: lse_over_noise(): total = lax.psum(jnp.sum(jnp.exp(scores - peak[None, :]), axis=0), 'row')]
    pmax x4 -> x0, blocking collectives: 248 us -> none  [the longest x2 156 us: lse_over_noise(): peak = lax.pmax(local_peak, 'row')]
    reduce_scatter x1 -> x0, waiting for transfers between devices: 167 us -> none  [per_device(): lax.psum_scatter(partial_value.astype(jnp.bfloat16), 'col', scatter_dimen...]
    all_gather x2 -> x0, waiting for transfers between devices: 158 us -> none  [the longest x1 90.7 us: per_device(): noise_full = lax.all_gather(noise, 'col', axis=1, tiled=True)]
    pallas_call x0 -> x1, Pallas kernels: none -> 69 us  [per_device(): pl.pallas_call(functools.partial(kernel, width), out_shape=(jax.ShapeDtyp...]
  transfers between devices with their start and end apart: 3 -> 0, of which waited for: 3 -> 0; matrix products, arithmetic and copies ran while one was open for 0% -> 0% of each run, Pallas kernels for 0% -> 0%
where the time goes in v2:
time: 73 us; the launch traced here: 72.2 us
  Pallas kernels  69 us (95%)
  local copies, waits for them, and re-layouts  2.59 us (4%)
    pallas_call x1, Pallas kernels, per_device(): pl.pallas_call(functools.partial(kernel, width), out_shape=(jax.ShapeDtyp...  69 us
    unnamed x7, local copies, waits for them, and re-layouts  2.59 us

profile of v2, /device:TPU:1, one launch (start us, length us, event | category | flops | bytes accessed | tf_op | source)
XLA Modules:
  0.0 72.2 jit_solution(10974015916461225428)
XLA Ops:
  0.6 69.0 %shard_map.67 = (bf16[16,8,256]{2,1,0:T(8,128)(2,1)}, f32[1,8]{1,0:T(1,128)}, f32[1,32]{1,0:T(1,128)}) custom-call(s32[8]{0:T(128)} %nw_hbm.1, s32[32]{0:T(128)} %dw_hbm.1, bf16[8,4096]{1,0:T(8,128)(2,1)} %noise_ref.1, bf16[32,2048]{1,0:T(8,128)(2,1)} %data_ref.1), custom_call_target="tpu_custom_call" | custom-call | tf_op jit(solution)/shard_map/pallas_call | solution.py:404
  69.6 0.0 copy-start.1
  69.6 1.5 %copy.10 = bf16[8,4096]{1,0:T(8,128)(2,1)} copy(bf16[8,4096]{1,0:T(8,128)(2,1)} %bitcast.5) | data formatting | bytes 131072
  71.1 0.0 copy-done.1
  71.1 0.0 copy-start
  71.1 0.5 copy.11
  71.6 0.1 copy-done
  71.7 0.5 copy.12
Async XLA Ops:
  69.6 1.5 %copy-start.1 = (f32[1,8]{1,0:T(1,128)S(1)}, f32[1,8]{1,0:T(1,128)}, u32[]{:S(2)}) copy-start(f32[1,8]{1,0:T(1,128)} %get-tuple-element.7) | copy-start | bytes 100
  71.1 0.6 copy-start

commit v3 on v2

--- a/solution.py
+++ b/solution.py
@@ -24,14 +24,13 @@
     width,
     nw_hbm, dw_hbm, noise_ref, data_ref,
     out_ref, npot_ref, dpot_ref,
-    nw_ref, dw_ref, nstage, dvm, dstage, wstage, nbuf, nmat, dcrit, dbuf, wbuf,
-    pbuf, abuf, bbuf, rbuf, gall, lbuf, vbuf, plan, tbuf,
-    load, ns, nr, cs, cr, ts, tr, ws, wr, sib_s, sib_r, as_, ar, bs, br,
-    gs, gr, hs, hr, os_, or_,
+    nw_ref, dw_ref, nstage, dvm, dstage, relay, wstage, nbuf, nmat, dcrit, tdata, dfull,
+    wbuf, pbuf, abuf, bbuf, rbuf, gall, lbuf, vbuf, plan, tbuf,
+    load, n1s, n1r, n2s, n2r, es, er, fs, fr, ts, tr, w1s, w1r, w2s, w2r, sib_s, sib_r,
+    as_, ar, bs, br, gs, gr, hs, hr, os_, or_,
 ):
     FQ = width // (Q * C)
     FS = X * FQ
-    half = C // 2
     eps = 1.0 / math.sqrt(width)
     row = lax.axis_index("row")
     c = lax.axis_index("col")
@@ -49,39 +48,41 @@
 
     sibling = (place(yl, x, other), c)
 
-    def data_target(j):
-        return (k * half + j) * 2 + c // half, q
-
-    source_row = c * 2 + yl // 2
-    to_self = jnp.logical_and(source_row == row, c // half == k)
+    def relay_of(j):
+        return place(2 * k + j // X, j % X, yh), z * YH + x % YH
+
+    def relay_source(i):
+        f = YH * i + yh
+        return place(f // X, f % X, yl // 2), z * YH + k
+
+    to_self = jnp.logical_and(jnp.logical_and(k == yl // 2, yh == k), x % YH == yh)
     n_self = jnp.where(to_self, 1, 0).astype(jnp.int32)
 
     def finish():
         def sent(ref, sem):
             pltpu.make_async_copy(ref, ref, sem).wait()
 
-        def sent_targets(ref, sem):
-            @pl.when(to_self)
-            def _():
-                sent(ref.at[pl.ds(0, half - 1)], sem)
-
-            @pl.when(jnp.logical_not(to_self))
-            def _():
-                sent(ref.at[pl.ds(0, half)], sem)
-
-        sent_targets(dstage, cs)
-        sent_targets(dbuf, ts)
-        sent_targets(wbuf, ws)
-        sent(nbuf.at[k, pl.ds(0, Q - 1)], ns)
+        @pl.when(to_self)
+        def _():
+            sent(dstage.at[pl.ds(0, 2 * X - 1)], es)
+
+        @pl.when(jnp.logical_not(to_self))
+        def _():
+            sent(dstage, es)
+
+        sent(relay.at[pl.ds(0, Z - 1)], fs)
+        sent(nstage.at[pl.ds(0, YL - 1)], n1s)
+        sent(nbuf.at[k, pl.ds(0, X - 1)], n2s)
         sent(nbuf.at[k], sib_s.at[0])
+        sent(wbuf.at[pl.ds(0, Z - 1), 0], w1s)
+        sent(wbuf.at[:, yh], w2s)
         sent(pbuf.at[pl.ds(0, Y - 1)], as_)
+        sent(tdata.at[pl.ds(0, 2 * X - 1)], ts)
         sent(rbuf.at[pl.ds(0, Z - 1)], bs)
-        sent(dbuf.at[pl.ds(0, half)], sib_s.at[1])
-        sent(wbuf.at[pl.ds(0, half)], sib_s.at[2])
         sent(gall.at[k, x, pl.ds(0, Y - 1)], gs)
         sent(gall.at[k, pl.ds(0, X - 1)], hs)
-        sent(gall.at[k], sib_s.at[3])
-        sent(tbuf.at[pl.ds(0, Q - 1)], os_)
+        sent(gall.at[k], sib_s.at[1])
+        sent(out_ref.at[pl.ds(0, Q - 1)], os_)
         sent(out_ref, or_)
 
     loads = [
@@ -100,13 +101,17 @@
     def greet(device):
         pl.semaphore_signal(barrier, inc=1, device_id=device, device_id_type=MESH)
 
-    def greet_source(j, carry):
-        sc = k * half + j
-
-        @pl.when(jnp.logical_or(source_row != row, sc != c))
-        def _():
-            greet((source_row, sc))
-
+    def greet_source(i, carry):
+        device = relay_source(i)
+
+        @pl.when(jnp.logical_or(device[0] != row, device[1] != c))
+        def _():
+            greet(device)
+
+        return carry
+
+    def greet_core(t, carry):
+        greet((place(yl, t, other), c))
         return carry
 
     def greet_z(s, carry):
@@ -121,11 +126,11 @@
         greet((lax.rem(q + s, Q) * 2 + k, c))
         return carry
 
-    lax.fori_loop(0, half, greet_source, 0)
+    lax.fori_loop(0, Z, greet_source, 0)
     lax.fori_loop(1, Z, greet_z, 0)
     lax.fori_loop(0, YL, greet_y, 0)
     lax.fori_loop(1, Q, greet_row, 0)
-    greet(sibling)
+    lax.fori_loop(0, X, greet_core, 0)
     for copy in loads:
         copy.start()
 
@@ -134,13 +139,9 @@
 
     for j in range(2 * X):
         s, t = j // X, j % X
-        dstage[j] = jnp.concatenate(
-            [
-                dvm[:, s * FS + f * FQ:s * FS + (f + 1) * FQ].astype(F32)[8 * t:8 * t + 8]
-                for f in range(X)
-            ],
-            axis=0,
-        ).astype(BF16)
+        for f in range(X):
+            cut = dvm[:, s * FS + f * FQ:s * FS + (f + 1) * FQ].astype(F32)
+            dstage[j, f] = cut[8 * t:8 * t + 8].astype(BF16)
     rows32 = lax.broadcasted_iota(jnp.int32, (32, LANES), 0)
     data_w = jnp.zeros((32, LANES), jnp.int32)
     for i in range(32):
@@ -165,44 +166,49 @@
         tail = jnp.where(lanes8 == 0, hi, tail)
         nstage[t, :, FS:FS + LANES] = tail.astype(BF16)
 
-    pl.semaphore_wait(barrier, (Q - 1) + (Z - 1) + YL + 1 + half - n_self)
-
-    def to_targets(src_of, dst, send, recv):
-        def step(j, carry):
-            device = data_target(j)
-            is_self = jnp.logical_and(device[0] == row, device[1] == c)
-
-            @pl.when(is_self)
-            def _():
-                pltpu.make_async_copy(src_of(j), dst, recv).start()
-
-            @pl.when(jnp.logical_not(is_self))
-            def _():
-                pltpu.make_async_remote_copy(
-                    src_of(j), dst, send, recv, device_id=device, device_id_type=MESH
-                ).start()
-
-            return carry
-
-        lax.fori_loop(0, half, step, 0)
-
-    to_targets(lambda j: dstage.at[j], dcrit.at[c % half], cs, cr)
-
-    def send_noise(s, carry):
-        t = lax.rem(q + s, Q)
-        pltpu.make_async_remote_copy(
-            nstage.at[t // X], nbuf.at[k, q], ns, nr,
-            device_id=(t * 2 + k, c), device_id_type=MESH,
-        ).start()
-        return carry
-
-    lax.fori_loop(1, Q, send_noise, 0)
-    pltpu.make_async_copy(nstage.at[yl], nbuf.at[k, q], nr).start()
-
-    to_targets(
-        lambda j: data_ref.at[:, pl.ds(pl.multiple_of(j * FQ, FQ), FQ)], dbuf.at[c], ts, tr
-    )
-    to_targets(lambda j: wstage, wbuf.at[c], ws, wr)
+    pl.semaphore_wait(barrier, (Q - 1) + X + (Z - 1) + YL + 2 * X - n_self)
+
+    def send_data(j, carry):
+        device = relay_of(j)
+        is_self = jnp.logical_and(device[0] == row, device[1] == c)
+        slot = q // YH
+
+        @pl.when(is_self)
+        def _():
+            pltpu.make_async_copy(dstage.at[j], relay.at[slot], er.at[slot]).start()
+
+        @pl.when(jnp.logical_not(is_self))
+        def _():
+            pltpu.make_async_remote_copy(
+                dstage.at[j], relay.at[slot], es, er.at[slot],
+                device_id=device, device_id_type=MESH,
+            ).start()
+
+        return carry
+
+    lax.fori_loop(0, 2 * X, send_data, 0)
+
+    def send_noise_y(s, carry):
+        t = lax.rem(yl + s, YL)
+        pltpu.make_async_remote_copy(
+            nstage.at[t], nbuf.at[k, x, yl], n1s, n1r,
+            device_id=(place(t, x, k), c), device_id_type=MESH,
+        ).start()
+        return carry
+
+    lax.fori_loop(1, YL, send_noise_y, 0)
+    pltpu.make_async_copy(nstage.at[yl], nbuf.at[k, x, yl], n1r).start()
+
+    def send_w(s, carry):
+        t = lax.rem(z + s, Z)
+        pltpu.make_async_remote_copy(
+            wstage, wbuf.at[z, yh], w1s, w1r,
+            device_id=(row, t * YH + yh), device_id_type=MESH,
+        ).start()
+        return carry
+
+    lax.fori_loop(1, Z, send_w, 0)
+    pltpu.make_async_copy(wstage, wbuf.at[z, yh], w1r).start()
 
     def arrived(ref, sem):
         pltpu.make_async_copy(ref, ref, sem).wait()
@@ -212,12 +218,43 @@
             ref, ref, sib_s.at[i], sib_r.at[i], device_id=sibling, device_id_type=MESH
         )
 
+    arrived(nbuf.at[k, x], n1r)
+
+    def send_noise_x(s, carry):
+        t = lax.rem(x + s, X)
+        pltpu.make_async_remote_copy(
+            nbuf.at[k, x], nbuf.at[k, x], n2s, n2r,
+            device_id=(place(yl, t, k), c), device_id_type=MESH,
+        ).start()
+        return carry
+
+    lax.fori_loop(1, X, send_noise_x, 0)
+
+    def hand_on(i, carry):
+        t = lax.rem(YH * yl + i, Z)
+        arrived(relay.at[t], er.at[t])
+
+        @pl.when(t == z)
+        def _():
+            pltpu.make_async_copy(relay.at[t], dcrit.at[z], fr).start()
+
+        @pl.when(t != z)
+        def _():
+            pltpu.make_async_remote_copy(
+                relay.at[t], dcrit.at[z], fs, fr,
+                device_id=(row, t * YH + yh), device_id_type=MESH,
+            ).start()
+
+        return carry
+
+    lax.fori_loop(0, Z, hand_on, 0)
+
     def noise_rows(core):
         for t in range(2):
-            part = nbuf[core, t * (Q // 2):(t + 1) * (Q // 2)].astype(F32)
+            part = nbuf[core, 2 * t:2 * t + 2].astype(F32)
             nmat[core, t * 4 * Q:(t + 1) * 4 * Q, :] = part.reshape(4 * Q, FS + LANES).astype(BF16)
 
-    arrived(nbuf.at[k], nr)
+    arrived(nbuf.at[k, pl.ds(0, X - 1)], n2r)
     noise_swap = swap(nbuf.at[k], 0)
     noise_swap.start()
     noise_rows(k)
@@ -229,15 +266,21 @@
     nsq = lax.dot_general(pick_sq, tail, NT, preferred_element_type=F32)[0:1, :]
     wa = lax.dot_general(pick_w, tail, NT, preferred_element_type=F32)[0:1, :]
 
-    arrived(dcrit, cr)
-    df = dcrit[...].astype(F32).reshape(half, X, 8, FQ)
+    arrived(wbuf.at[:, yh], w1r)
+    pltpu.make_async_remote_copy(
+        wbuf.at[:, yh], wbuf.at[:, yh], w2s, w2r,
+        device_id=(row, z * YH + 1 - yh), device_id_type=MESH,
+    ).start()
+
+    arrived(dcrit, fr)
+    df = dcrit[...].astype(F32)
     part = jnp.sum(
-        jnp.sum(df * df, axis=1).reshape(half * 8, FQ), axis=1, keepdims=True
+        jnp.sum(df * df, axis=1).reshape(Z * 8, FQ), axis=1, keepdims=True
     ) + nsq
     dm = (df * -2.0)
     for f in range(X):
         part = part + lax.dot_general(
-            dm[:, f].reshape(half * 8, FQ).astype(BF16),
+            dm[:, f].reshape(Z * 8, FQ).astype(BF16),
             nmat[:, :, f * FQ:(f + 1) * FQ].reshape(16 * Q, FQ),
             NT, preferred_element_type=F32,
         )
@@ -256,6 +299,18 @@
 
     lax.fori_loop(1, Y, send_a, 0)
     pltpu.make_async_copy(pbuf.at[y], abuf.at[y], ar).start()
+
+    def send_features(j, carry):
+        t, core = lax.rem(x + j // 2, X), lax.rem(k + j, 2)
+        pltpu.make_async_remote_copy(
+            dcrit.at[:, t], tdata.at[:, k * X + x], ts, tr,
+            device_id=(place(yl, t, core), c), device_id_type=MESH,
+        ).start()
+        return carry
+
+    lax.fori_loop(1, 2 * X, send_features, 0)
+    pltpu.make_async_copy(dcrit.at[:, x], tdata.at[:, k * X + x], tr).start()
+
     log_a = jnp.log(wa / jnp.sum(wa, axis=1, keepdims=True))
     log_a = [log_a[:, h * LANES:(h + 1) * LANES] for h in range(2)]
     arrived(abuf, ar)
@@ -274,15 +329,6 @@
     lax.fori_loop(1, Z, send_b, 0)
     pltpu.make_async_copy(bbuf, rbuf.at[z], br).start()
 
-    own_data = dbuf.at[pl.ds(k * half, half)]
-    arrived(own_data, tr)
-    data_swap = swap(own_data, 1)
-    data_swap.start()
-    own_w = wbuf.at[pl.ds(k * half, half)]
-    arrived(own_w, wr)
-    w_swap = swap(own_w, 2)
-    w_swap.start()
-
     arrived(rbuf, br)
     total = rbuf[0]
     for j in range(1, Z):
@@ -299,12 +345,16 @@
 
     lax.fori_loop(1, Y, send_g, 0)
 
-    arrived(wbuf.at[pl.ds(other * half, half)], sib_r.at[2])
-    wb = wbuf[...].astype(F32)
-    w_sum = jnp.sum(jnp.sum(wb, axis=0), axis=0, keepdims=True)
-    log_b = jnp.log(wb / w_sum).reshape(2, half, X, 8, LANES)
-    for t in range(X):
-        lbuf[:, t] = log_b[:, :, t]
+    arrived(wbuf.at[:, 1 - yh], w2r)
+    wb = wbuf[...].astype(F32).reshape(Z, YH, X, 8, LANES)
+    w_sum = jnp.sum(jnp.sum(wb, axis=(0, 1, 2)), axis=0, keepdims=True)
+    log_b = jnp.log(wb / w_sum)
+    for a in range(YH):
+        for b in range(X):
+            lbuf[a, b] = log_b[:, a, b]
+    arrived(tdata, tr)
+    for t in range(Z):
+        dfull[t * 64:(t + 1) * 64, :] = tdata[t].astype(F32).reshape(64, FQ).astype(BF16)
 
     arrived(gall.at[k, x, pl.ds(0, Y - 1)], gr)
 
@@ -318,9 +368,9 @@
 
     lax.fori_loop(1, X, send_h, 0)
     arrived(gall.at[k, pl.ds(0, X - 1)], hr)
-    cost_swap = swap(gall.at[k], 3)
+    cost_swap = swap(gall.at[k], 1)
     cost_swap.start()
-    arrived(gall.at[other], sib_r.at[3])
+    arrived(gall.at[other], sib_r.at[1])
 
     def parts(i):
         return i // X, i % X
@@ -359,36 +409,35 @@
     own_u = jnp.where(k == 0, u[0], u[1])
     for i in range(2 * X):
         a, b = parts(i)
-        plan[a, :, b] = jnp.exp(gall[a, b, :, k] + own_u + vbuf[a, b])
+        plan[:, a, b] = jnp.exp(gall[a, b, :, k] + own_u + vbuf[a, b])
     p = jnp.transpose(plan[...].reshape(C * 32, LANES), (1, 0))
     mass = jnp.sum(p, axis=1, keepdims=True)
 
-    arrived(dbuf.at[pl.ds(other * half, half)], sib_r.at[1])
     value = jnp.dot(
-        p.astype(BF16), dbuf[...].reshape(C * 32, FQ), preferred_element_type=F32
+        p.astype(BF16), dfull[...], preferred_element_type=F32
     ) / mass
-    tbuf[...] = value.reshape(Q, 8, FQ).astype(BF16)
+    tbuf[...] = value.reshape(X, YL, 8, FQ).astype(BF16)
 
     def send_t(s, carry):
         t = lax.rem(q + s, Q)
         pltpu.make_async_remote_copy(
-            tbuf.at[t], out_ref.at[q], os_, or_,
+            tbuf.at[t % X, t // X], out_ref.at[q], os_, or_,
             device_id=(t * 2 + k, c), device_id_type=MESH,
         ).start()
         return carry
 
     lax.fori_loop(1, Q, send_t, 0)
-    pltpu.make_async_copy(tbuf.at[q], out_ref.at[q], or_).start()
+    pltpu.make_async_copy(tbuf.at[x, yl], out_ref.at[q], or_).start()
 
     mine = own_u[:, 0:8]
     for t in range(1, Q):
-        mine = jnp.where(q == t, own_u[:, 8 * t:8 * t + 8], mine)
+        mine = jnp.where(x * YL + yl == t, own_u[:, 8 * t:8 * t + 8], mine)
     npot_ref[...] = mine * eps
     lanes4 = lax.broadcasted_iota(jnp.int32, (X, 8, LANES), 2)
     index4 = lax.broadcasted_iota(jnp.int32, (X, 8, LANES), 0) * 8 + lax.broadcasted_iota(
         jnp.int32, (X, 8, LANES), 1
     )
-    block = jnp.where(lanes4 == index4, vbuf[c // half, :, c % half], 0.0)
+    block = jnp.where(lanes4 == index4, vbuf[yh, :, z], 0.0)
     block = jnp.sum(jnp.sum(block, axis=0), axis=0, keepdims=True)
     dpot_ref[...] = block[:, 0:32] * eps
     finish()
@@ -415,13 +464,15 @@
             pltpu.SMEM((32,), jnp.int32),
             pltpu.VMEM((YL, 8, FS + LANES), BF16),
             pltpu.VMEM((32, 2 * FS), BF16),
-            pltpu.VMEM((2 * X, 32, FQ), BF16),
+            pltpu.VMEM((2 * X, X, 8, FQ), BF16),
+            pltpu.VMEM((Z, X, 8, FQ), BF16),
             pltpu.VMEM((32, LANES), BF16),
-            pltpu.VMEM((2, Q, 8, FS + LANES), BF16),
+            pltpu.VMEM((2, X, YL, 8, FS + LANES), BF16),
             pltpu.VMEM((2, 8 * Q, FS + LANES), BF16),
-            pltpu.VMEM((C // 2, 32, FQ), BF16),
-            pltpu.VMEM((C, 32, FQ), BF16),
-            pltpu.VMEM((C, 32, LANES), BF16),
+            pltpu.VMEM((Z, X, 8, FQ), BF16),
+            pltpu.VMEM((Z, 2 * X, 8, FQ), BF16),
+            pltpu.VMEM((C * 32, FQ), BF16),
+            pltpu.VMEM((Z, YH, 32, LANES), BF16),
             pltpu.VMEM((Y, 2, 8, LANES), F32),
             pltpu.VMEM((Y, 2, 8, LANES), F32),
             pltpu.VMEM((2, 8, LANES), F32),
@@ -429,10 +480,10 @@
             pltpu.VMEM((2, X, Y, 2, 8, LANES), F32),
             pltpu.VMEM((2, X, Y, 8, LANES), F32),
             pltpu.VMEM((2, X, Y, 8, LANES), F32),
-            pltpu.VMEM((2, Y, X, 8, LANES), F32),
-            pltpu.VMEM((Q, 8, FQ), BF16),
+            pltpu.VMEM((Z, 2, X, 8, LANES), F32),
+            pltpu.VMEM((X, YL, 8, FQ), BF16),
             dma((3 + YL,)),
-        ] + [dma] * 8 + [dma((4,))] * 2 + [dma] * 10,
+        ] + [dma] * 5 + [dma((Z,))] + [dma] * 8 + [dma((2,))] * 2 + [dma] * 10,
         compiler_params=pltpu.CompilerParams(
             collective_id=0, has_side_effects=True, vmem_limit_bytes=60 * 1024 * 1024
         ),

time: 73 us -> 64.7 us (0.89)
  Pallas kernels: 69 us -> 61.3 us
    pallas_call x1, Pallas kernels: 69 us -> 61.3 us  [per_device(): pl.pallas_call(functools.partial(kernel, width), out_shape=(jax.ShapeDtyp...]
where the time goes in v3:
time: 64.7 us; the launch traced here: 64.5 us
  Pallas kernels  61.3 us (95%)
  local copies, waits for them, and re-layouts  2.59 us (4%)
  between operations  0.65 us (1%)
    pallas_call x1, Pallas kernels, per_device(): pl.pallas_call(functools.partial(kernel, width), out_shape=(jax.ShapeDtyp...  61.3 us
    unnamed x7, local copies, waits for them, and re-layouts  2.59 us

profile of v3, /device:TPU:1, one launch (start us, length us, event | category | flops | bytes accessed | tf_op | source)
XLA Modules:
  0.0 64.5 jit_solution(2797581194602207691)
XLA Ops:
  0.6 61.3 %shard_map.67 = (bf16[16,8,256]{2,1,0:T(8,128)(2,1)}, f32[1,8]{1,0:T(1,128)}, f32[1,32]{1,0:T(1,128)}) custom-call(s32[8]{0:T(128)} %nw_hbm.1, s32[32]{0:T(128)} %dw_hbm.1, bf16[8,4096]{1,0:T(8,128)(2,1)} %noise_ref.1, bf16[32,2048]{1,0:T(8,128)(2,1)} %data_ref.1), custom_call_target="tpu_custom_call" | custom-call | tf_op jit(solution)/shard_map/pallas_call | solution.py:453
  61.9 0.0 copy-start.1
  61.9 1.5 %copy.10 = bf16[8,4096]{1,0:T(8,128)(2,1)} copy(bf16[8,4096]{1,0:T(8,128)(2,1)} %bitcast.5) | data formatting | bytes 131072
  63.4 0.0 copy-done.1
  63.4 0.0 copy-start
  63.4 0.5 copy.11
  63.9 0.1 copy-done
  64.0 0.5 copy.12
Async XLA Ops:
  61.9 1.5 %copy-start.1 = (f32[1,8]{1,0:T(1,128)S(1)}, f32[1,8]{1,0:T(1,128)}, u32[]{:S(2)}) copy-start(f32[1,8]{1,0:T(1,128)} %get-tuple-element.7) | copy-start | bytes 100
  63.4 0.6 copy-start

commit v4 on v3

--- a/solution.py
+++ b/solution.py
@@ -142,11 +142,11 @@
         for f in range(X):
             cut = dvm[:, s * FS + f * FQ:s * FS + (f + 1) * FQ].astype(F32)
             dstage[j, f] = cut[8 * t:8 * t + 8].astype(BF16)
-    rows32 = lax.broadcasted_iota(jnp.int32, (32, LANES), 0)
-    data_w = jnp.zeros((32, LANES), jnp.int32)
+    lanes1 = lax.broadcasted_iota(jnp.int32, (1, LANES), 1)
+    data_w = jnp.zeros((1, LANES), jnp.int32)
     for i in range(32):
-        data_w = jnp.where(rows32 == i, dw_ref[i], data_w)
-    wstage[...] = data_w.astype(F32).astype(BF16)
+        data_w = jnp.where(lanes1 == i, dw_ref[i], data_w)
+    wstage[...] = data_w.astype(F32)
 
     rows8 = lax.broadcasted_iota(jnp.int32, (8, LANES), 0)
     lanes8 = lax.broadcasted_iota(jnp.int32, (8, LANES), 1)
@@ -338,17 +338,32 @@
     def send_g(s, carry):
         t = lax.rem(y + s, Y)
         pltpu.make_async_remote_copy(
-            gall.at[k, x, y], gall.at[k, x, y], gs, gr,
+            gall.at[k, x, y], gall.at[k, x, y], gs, gr.at[y],
             device_id=y_peer(t), device_id_type=MESH,
         ).start()
         return carry
 
     lax.fori_loop(1, Y, send_g, 0)
 
+    def send_x(piece):
+        for s in range(1, X):
+            t = lax.rem(x + s, X)
+            pltpu.make_async_remote_copy(
+                gall.at[k, x, piece], gall.at[k, x, piece], hs, hr.at[x],
+                device_id=(place(yl, t, k), c), device_id_type=MESH,
+            ).start()
+
+    send_x(y)
+
     arrived(wbuf.at[:, 1 - yh], w2r)
-    wb = wbuf[...].astype(F32).reshape(Z, YH, X, 8, LANES)
-    w_sum = jnp.sum(jnp.sum(wb, axis=(0, 1, 2)), axis=0, keepdims=True)
-    log_b = jnp.log(wb / w_sum)
+    wb = wbuf[...].reshape(C, 1, LANES)
+    w_sum = jnp.sum(jnp.sum(wb, axis=0), axis=1, keepdims=True)
+    spot = lax.broadcasted_iota(jnp.int32, (C, 32, LANES), 1) == lax.broadcasted_iota(
+        jnp.int32, (C, 32, LANES), 2
+    )
+    wb = jnp.where(spot, wb, 0.0).reshape(C * 32, LANES).astype(BF16)
+    wb = jnp.dot(wb, jnp.ones((LANES, LANES), BF16), preferred_element_type=F32)
+    log_b = jnp.log(wb / w_sum).reshape(Z, YH, X, 8, LANES)
     for a in range(YH):
         for b in range(X):
             lbuf[a, b] = log_b[:, a, b]
@@ -356,20 +371,30 @@
     for t in range(Z):
         dfull[t * 64:(t + 1) * 64, :] = tdata[t].astype(F32).reshape(64, FQ).astype(BF16)
 
-    arrived(gall.at[k, x, pl.ds(0, Y - 1)], gr)
-
-    def send_h(s, carry):
-        t = lax.rem(x + s, X)
-        pltpu.make_async_remote_copy(
-            gall.at[k, x], gall.at[k, x], hs, hr,
-            device_id=(place(yl, t, k), c), device_id_type=MESH,
-        ).start()
-        return carry
-
-    lax.fori_loop(1, X, send_h, 0)
-    arrived(gall.at[k, pl.ds(0, X - 1)], hr)
-    cost_swap = swap(gall.at[k], 1)
-    cost_swap.start()
+    def gather_y(i, carry):
+        d = (i + 1) // 2
+        t = lax.rem(y + jnp.where(i % 2 == 1, d, Y - d), Y)
+        arrived(gall.at[k, x, t], gr.at[t])
+        send_x(t)
+        return carry
+
+    lax.fori_loop(1, Y, gather_y, 0)
+
+    def send_core(t):
+        pltpu.make_async_remote_copy(
+            gall.at[k, t], gall.at[k, t], sib_s.at[1], sib_r.at[1],
+            device_id=sibling, device_id_type=MESH,
+        ).start()
+
+    send_core(x)
+
+    def gather_x(s, carry):
+        t = lax.rem(x + jnp.where(s == 2, 3, jnp.where(s == 3, 2, 1)), X)
+        arrived(gall.at[k, t], hr.at[t])
+        send_core(t)
+        return carry
+
+    lax.fori_loop(1, X, gather_x, 0)
     arrived(gall.at[other], sib_r.at[1])
 
     def parts(i):
@@ -466,13 +491,13 @@
             pltpu.VMEM((32, 2 * FS), BF16),
             pltpu.VMEM((2 * X, X, 8, FQ), BF16),
             pltpu.VMEM((Z, X, 8, FQ), BF16),
-            pltpu.VMEM((32, LANES), BF16),
+            pltpu.VMEM((1, LANES), F32),
             pltpu.VMEM((2, X, YL, 8, FS + LANES), BF16),
             pltpu.VMEM((2, 8 * Q, FS + LANES), BF16),
             pltpu.VMEM((Z, X, 8, FQ), BF16),
             pltpu.VMEM((Z, 2 * X, 8, FQ), BF16),
             pltpu.VMEM((C * 32, FQ), BF16),
-            pltpu.VMEM((Z, YH, 32, LANES), BF16),
+            pltpu.VMEM((Z, YH, 1, LANES), F32),
             pltpu.VMEM((Y, 2, 8, LANES), F32),
             pltpu.VMEM((Y, 2, 8, LANES), F32),
             pltpu.VMEM((2, 8, LANES), F32),
@@ -483,7 +508,7 @@
             pltpu.VMEM((Z, 2, X, 8, LANES), F32),
             pltpu.VMEM((X, YL, 8, FQ), BF16),
             dma((3 + YL,)),
-        ] + [dma] * 5 + [dma((Z,))] + [dma] * 8 + [dma((2,))] * 2 + [dma] * 10,
+        ] + [dma] * 5 + [dma((Z,))] + [dma] * 8 + [dma((2,))] * 2 + [dma] * 5 + [dma((Y,)), dma, dma((X,)), dma, dma],
         compiler_params=pltpu.CompilerParams(
             collective_id=0, has_side_effects=True, vmem_limit_bytes=60 * 1024 * 1024
         ),

time: 64.7 us -> 61.3 us (0.947)
  Pallas kernels: 61.3 us -> 57.9 us
    pallas_call x1, Pallas kernels: 61.3 us -> 57.9 us  [per_device(): pl.pallas_call(functools.partial(kernel, width), out_shape=(jax.ShapeDtyp...]
where the time goes in v4:
time: 61.3 us; the launch traced here: 61.2 us
  Pallas kernels  57.9 us (94%)
  local copies, waits for them, and re-layouts  2.59 us (4%)
  between operations  0.65 us (1%)
    pallas_call x1, Pallas kernels, per_device(): pl.pallas_call(functools.partial(kernel, width), out_shape=(jax.ShapeDtyp...  57.9 us
    unnamed x7, local copies, waits for them, and re-layouts  2.59 us

profile of v4, /device:TPU:1, one launch (start us, length us, event | category | flops | bytes accessed | tf_op | source)
XLA Modules:
  0.0 61.2 jit_solution(11394875754986223174)
XLA Ops:
  0.6 57.9 %shard_map.67 = (bf16[16,8,256]{2,1,0:T(8,128)(2,1)}, f32[1,8]{1,0:T(1,128)}, f32[1,32]{1,0:T(1,128)}) custom-call(s32[8]{0:T(128)} %nw_hbm.1, s32[32]{0:T(128)} %dw_hbm.1, bf16[8,4096]{1,0:T(8,128)(2,1)} %noise_ref.1, bf16[32,2048]{1,0:T(8,128)(2,1)} %data_ref.1), custom_call_target="tpu_custom_call" | custom-call | tf_op jit(solution)/shard_map/pallas_call | solution.py:478
  58.6 0.0 copy-start.1
  58.6 1.5 %copy.10 = bf16[8,4096]{1,0:T(8,128)(2,1)} copy(bf16[8,4096]{1,0:T(8,128)(2,1)} %bitcast.5) | data formatting | bytes 131072
  60.0 0.0 copy-done.1
  60.0 0.0 copy-start
  60.0 0.5 copy.11
  60.6 0.1 copy-done
  60.6 0.5 copy.12
Async XLA Ops:
  58.6 1.5 %copy-start.1 = (f32[1,8]{1,0:T(1,128)S(1)}, f32[1,8]{1,0:T(1,128)}, u32[]{:S(2)}) copy-start(f32[1,8]{1,0:T(1,128)} %get-tuple-element.7) | copy-start | bytes 100
  60.0 0.6 copy-start

commit v5 on v4

--- a/solution.py
+++ b/solution.py
@@ -126,27 +126,47 @@
         greet((lax.rem(q + s, Q) * 2 + k, c))
         return carry
 
+    for copy in loads[2::-1]:
+        copy.start()
     lax.fori_loop(0, Z, greet_source, 0)
     lax.fori_loop(1, Z, greet_z, 0)
     lax.fori_loop(0, YL, greet_y, 0)
     lax.fori_loop(1, Q, greet_row, 0)
     lax.fori_loop(0, X, greet_core, 0)
-    for copy in loads:
+    for copy in loads[3:]:
         copy.start()
 
-    for copy in loads:
-        copy.wait()
-
+    loads[2].wait()
     for j in range(2 * X):
         s, t = j // X, j % X
         for f in range(X):
             cut = dvm[:, s * FS + f * FQ:s * FS + (f + 1) * FQ].astype(F32)
             dstage[j, f] = cut[8 * t:8 * t + 8].astype(BF16)
-    lanes1 = lax.broadcasted_iota(jnp.int32, (1, LANES), 1)
-    data_w = jnp.zeros((1, LANES), jnp.int32)
-    for i in range(32):
-        data_w = jnp.where(lanes1 == i, dw_ref[i], data_w)
-    wstage[...] = data_w.astype(F32)
+    pl.semaphore_wait(barrier, (Q - 1) + X + (Z - 1) + YL + 2 * X - n_self)
+
+    def send_data(j, carry):
+        device = relay_of(j)
+        is_self = jnp.logical_and(device[0] == row, device[1] == c)
+        slot = q // YH
+
+        @pl.when(is_self)
+        def _():
+            pltpu.make_async_copy(dstage.at[j], relay.at[slot], er.at[slot]).start()
+
+        @pl.when(jnp.logical_not(is_self))
+        def _():
+            pltpu.make_async_remote_copy(
+                dstage.at[j], relay.at[slot], es, er.at[slot],
+                device_id=device, device_id_type=MESH,
+            ).start()
+
+        return carry
+
+    lax.fori_loop(0, 2 * X, send_data, 0)
+
+    loads[0].wait()
+    for copy in loads[3:]:
+        copy.wait()
 
     rows8 = lax.broadcasted_iota(jnp.int32, (8, LANES), 0)
     lanes8 = lax.broadcasted_iota(jnp.int32, (8, LANES), 1)
@@ -166,28 +186,6 @@
         tail = jnp.where(lanes8 == 0, hi, tail)
         nstage[t, :, FS:FS + LANES] = tail.astype(BF16)
 
-    pl.semaphore_wait(barrier, (Q - 1) + X + (Z - 1) + YL + 2 * X - n_self)
-
-    def send_data(j, carry):
-        device = relay_of(j)
-        is_self = jnp.logical_and(device[0] == row, device[1] == c)
-        slot = q // YH
-
-        @pl.when(is_self)
-        def _():
-            pltpu.make_async_copy(dstage.at[j], relay.at[slot], er.at[slot]).start()
-
-        @pl.when(jnp.logical_not(is_self))
-        def _():
-            pltpu.make_async_remote_copy(
-                dstage.at[j], relay.at[slot], es, er.at[slot],
-                device_id=device, device_id_type=MESH,
-            ).start()
-
-        return carry
-
-    lax.fori_loop(0, 2 * X, send_data, 0)
-
     def send_noise_y(s, carry):
         t = lax.rem(yl + s, YL)
         pltpu.make_async_remote_copy(
@@ -198,6 +196,13 @@
 
     lax.fori_loop(1, YL, send_noise_y, 0)
     pltpu.make_async_copy(nstage.at[yl], nbuf.at[k, x, yl], n1r).start()
+
+    loads[1].wait()
+    lanes1 = lax.broadcasted_iota(jnp.int32, (1, LANES), 1)
+    data_w = jnp.zeros((1, LANES), jnp.int32)
+    for i in range(32):
+        data_w = jnp.where(lanes1 == i, dw_ref[i], data_w)
+    wstage[...] = data_w.astype(F32)
 
     def send_w(s, carry):
         t = lax.rem(z + s, Z)
@@ -404,7 +409,9 @@
         a, b = parts(i)
         return jnp.maximum(peak, jnp.max(gall[a, b], axis=0))
 
-    peak = lax.fori_loop(0, 2 * X, peak_step, jnp.full((2, 8, LANES), -jnp.inf, F32))
+    peak = jnp.full((2, 8, LANES), -jnp.inf, F32)
+    for i in range(2 * X):
+        peak = peak_step(i, peak)
     for rounds in range(HALVES // 2):
         top = jnp.max(peak, axis=1, keepdims=True)
 
@@ -415,7 +422,9 @@
                 s = s + vbuf[a, b][:, None]
             return acc + jnp.sum(jnp.exp(s - top), axis=0)
 
-        acc = lax.fori_loop(0, 2 * X, noise_step, jnp.zeros((2, 8, LANES), F32))
+        acc = jnp.zeros((2, 8, LANES), F32)
+        for i in range(2 * X):
+            acc = noise_step(i, acc)
         lse = top + jnp.log(jnp.sum(acc, axis=1, keepdims=True))
         u = jnp.concatenate([(log_a[h] - lse[h])[None] for h in range(2)], axis=0)
 
@@ -429,7 +438,9 @@
             vbuf[a, b] = v
             return jnp.maximum(peak, jnp.max(s + v[:, None], axis=0))
 
-        peak = lax.fori_loop(0, 2 * X, data_step, jnp.full((2, 8, LANES), -jnp.inf, F32))
+        peak = jnp.full((2, 8, LANES), -jnp.inf, F32)
+        for i in range(2 * X):
+            peak = data_step(i, peak)
 
     own_u = jnp.where(k == 0, u[0], u[1])
     for i in range(2 * X):

time: 61.3 us -> 58.3 us (0.951)
  Pallas kernels: 57.9 us -> 54.9 us
    pallas_call x1, Pallas kernels: 57.9 us -> 54.9 us  [per_device(): pl.pallas_call(functools.partial(kernel, width), out_shape=(jax.ShapeDtyp...]
where the time goes in v5:
time: 58.3 us; the launch traced here: 58.1 us
  Pallas kernels  54.9 us (94%)
  local copies, waits for them, and re-layouts  2.59 us (4%)
  between operations  0.65 us (1%)
    pallas_call x1, Pallas kernels, per_device(): pl.pallas_call(functools.partial(kernel, width), out_shape=(jax.ShapeDtyp...  54.9 us
    unnamed x7, local copies, waits for them, and re-layouts  2.59 us

profile of v5, /device:TPU:1, one launch (start us, length us, event | category | flops | bytes accessed | tf_op | source)
XLA Modules:
  0.0 58.1 jit_solution(1030093692275115389)
XLA Ops:
  0.6 54.9 %shard_map.67 = (bf16[16,8,256]{2,1,0:T(8,128)(2,1)}, f32[1,8]{1,0:T(1,128)}, f32[1,32]{1,0:T(1,128)}) custom-call(s32[8]{0:T(128)} %nw_hbm.1, s32[32]{0:T(128)} %dw_hbm.1, bf16[8,4096]{1,0:T(8,128)(2,1)} %noise_ref.1, bf16[32,2048]{1,0:T(8,128)(2,1)} %data_ref.1), custom_call_target="tpu_custom_call" | custom-call | tf_op jit(solution)/shard_map/pallas_call | solution.py:489
  55.5 0.0 copy-start.1
  55.5 1.5 %copy.10 = bf16[8,4096]{1,0:T(8,128)(2,1)} copy(bf16[8,4096]{1,0:T(8,128)(2,1)} %bitcast.5) | data formatting | bytes 131072
  57.0 0.0 copy-done.1
  57.0 0.0 copy-start
  57.0 0.5 copy.11
  57.5 0.1 copy-done
  57.6 0.5 copy.12
Async XLA Ops:
  55.5 1.5 %copy-start.1 = (f32[1,8]{1,0:T(1,128)S(1)}, f32[1,8]{1,0:T(1,128)}, u32[]{:S(2)}) copy-start(f32[1,8]{1,0:T(1,128)} %get-tuple-element.7) | copy-start | bytes 100
  57.0 0.6 %copy-start = (f32[1,32]{1,0:T(1,128)S(1)}, f32[1,32]{1,0:T(1,128)}, u32[]{:S(2)}) copy-start(f32[1,32]{1,0:T(1,128)} %get-tuple-element.8) | copy-start | bytes 388

commit v6 on v5

--- a/solution.py
+++ b/solution.py
@@ -23,11 +23,11 @@
 def kernel(
     width,
     nw_hbm, dw_hbm, noise_ref, data_ref,
-    out_ref, npot_ref, dpot_ref,
+    out_ref, pots_ref,
     nw_ref, dw_ref, nstage, dvm, dstage, relay, wstage, nbuf, nmat, dcrit, tdata, dfull,
-    wbuf, pbuf, abuf, bbuf, rbuf, gall, lbuf, vbuf, plan, tbuf,
+    wbuf, pbuf, abuf, bbuf, rbuf, gall, lbuf, vbuf, plan, turned, tbuf, pots,
     load, n1s, n1r, n2s, n2r, es, er, fs, fr, ts, tr, w1s, w1r, w2s, w2r, sib_s, sib_r,
-    as_, ar, bs, br, gs, gr, hs, hr, os_, or_,
+    as_, ar, bs, br, gs, gr, hs, hr, os_, or_, ps,
 ):
     FQ = width // (Q * C)
     FS = X * FQ
@@ -77,13 +77,15 @@
         sent(wbuf.at[pl.ds(0, Z - 1), 0], w1s)
         sent(wbuf.at[:, yh], w2s)
         sent(pbuf.at[pl.ds(0, Y - 1)], as_)
-        sent(tdata.at[pl.ds(0, 2 * X - 1)], ts)
+        sent(tdata.at[pl.ds(0, X - 1)], ts)
         sent(rbuf.at[pl.ds(0, Z - 1)], bs)
         sent(gall.at[k, x, pl.ds(0, Y - 1)], gs)
         sent(gall.at[k, pl.ds(0, X - 1)], hs)
         sent(gall.at[k], sib_s.at[1])
-        sent(out_ref.at[pl.ds(0, Q - 1)], os_)
+        sent(tdata.at[pl.ds(0, X)], sib_s.at[2])
+        sent(out_ref.at[pl.ds(0, YL - 1)], os_)
         sent(out_ref, or_)
+        sent(pots_ref, ps)
 
     loads = [
         pltpu.make_async_copy(nw_hbm, nw_ref, load.at[0]),
@@ -110,29 +112,26 @@
 
         return carry
 
-    def greet_core(t, carry):
-        greet((place(yl, t, other), c))
-        return carry
-
     def greet_z(s, carry):
         greet((row, lax.rem(z + s, Z) * YH + yh))
         return carry
 
-    def greet_y(t, carry):
-        greet((place(t, x, k), z * YH + 1 - yh))
-        return carry
-
-    def greet_row(s, carry):
-        greet((lax.rem(q + s, Q) * 2 + k, c))
+    def greet_y(s, carry):
+        t = lax.rem(y + s, Y)
+        greet((place(t % YL, x, k), z * YH + t // YL))
+        return carry
+
+    def greet_x(s, carry):
+        greet((place(yl, lax.rem(x + s, X), k), c))
         return carry
 
     for copy in loads[2::-1]:
         copy.start()
     lax.fori_loop(0, Z, greet_source, 0)
     lax.fori_loop(1, Z, greet_z, 0)
-    lax.fori_loop(0, YL, greet_y, 0)
-    lax.fori_loop(1, Q, greet_row, 0)
-    lax.fori_loop(0, X, greet_core, 0)
+    lax.fori_loop(1, Y, greet_y, 0)
+    lax.fori_loop(1, X, greet_x, 0)
+    greet(sibling)
     for copy in loads[3:]:
         copy.start()
 
@@ -142,7 +141,7 @@
         for f in range(X):
             cut = dvm[:, s * FS + f * FQ:s * FS + (f + 1) * FQ].astype(F32)
             dstage[j, f] = cut[8 * t:8 * t + 8].astype(BF16)
-    pl.semaphore_wait(barrier, (Q - 1) + X + (Z - 1) + YL + 2 * X - n_self)
+    pl.semaphore_wait(barrier, (Y - 1) + (X - 1) + (Z - 1) + 1 + 2 * X - n_self)
 
     def send_data(j, carry):
         device = relay_of(j)
@@ -305,16 +304,16 @@
     lax.fori_loop(1, Y, send_a, 0)
     pltpu.make_async_copy(pbuf.at[y], abuf.at[y], ar).start()
 
-    def send_features(j, carry):
-        t, core = lax.rem(x + j // 2, X), lax.rem(k + j, 2)
-        pltpu.make_async_remote_copy(
-            dcrit.at[:, t], tdata.at[:, k * X + x], ts, tr,
-            device_id=(place(yl, t, core), c), device_id_type=MESH,
-        ).start()
-        return carry
-
-    lax.fori_loop(1, 2 * X, send_features, 0)
-    pltpu.make_async_copy(dcrit.at[:, x], tdata.at[:, k * X + x], tr).start()
+    def send_features(s, carry):
+        t = lax.rem(x + s, X)
+        pltpu.make_async_remote_copy(
+            dcrit, tdata.at[k * X + x], ts, tr,
+            device_id=(place(yl, t, k), c), device_id_type=MESH,
+        ).start()
+        return carry
+
+    lax.fori_loop(1, X, send_features, 0)
+    pltpu.make_async_copy(dcrit, tdata.at[k * X + x], tr).start()
 
     log_a = jnp.log(wa / jnp.sum(wa, axis=1, keepdims=True))
     log_a = [log_a[:, h * LANES:(h + 1) * LANES] for h in range(2)]
@@ -372,9 +371,22 @@
     for a in range(YH):
         for b in range(X):
             lbuf[a, b] = log_b[:, a, b]
-    arrived(tdata, tr)
-    for t in range(Z):
-        dfull[t * 64:(t + 1) * 64, :] = tdata[t].astype(F32).reshape(64, FQ).astype(BF16)
+    def data_rows(core):
+        def step(i, carry):
+            g = core * X + i
+            for f in range(X):
+                cut = tdata[g, :, f].astype(F32).reshape(Z * 8, FQ)
+                dfull[g, :, f * FQ:(f + 1) * FQ] = cut.astype(BF16)
+            return carry
+
+        lax.fori_loop(0, X, step, 0)
+
+    own_rows = tdata.at[pl.ds(k * X, X)]
+    other_rows = tdata.at[pl.ds(other * X, X)]
+    arrived(own_rows, tr)
+    rows_swap = swap(own_rows, 2)
+    rows_swap.start()
+    data_rows(k)
 
     def gather_y(i, carry):
         d = (i + 1) // 2
@@ -400,6 +412,8 @@
         return carry
 
     lax.fori_loop(1, X, gather_x, 0)
+    arrived(other_rows, sib_r.at[2])
+    data_rows(other)
     arrived(gall.at[other], sib_r.at[1])
 
     def parts(i):
@@ -442,40 +456,42 @@
         for i in range(2 * X):
             peak = data_step(i, peak)
 
+    pots[...] = jnp.zeros_like(pots)
     own_u = jnp.where(k == 0, u[0], u[1])
     for i in range(2 * X):
         a, b = parts(i)
-        plan[:, a, b] = jnp.exp(gall[a, b, :, k] + own_u + vbuf[a, b])
-    p = jnp.transpose(plan[...].reshape(C * 32, LANES), (1, 0))
+        plan[a, b] = jnp.exp(gall[a, b, :, k] + own_u + vbuf[a, b])
+    turned[...] = jnp.transpose(plan[...].reshape(C * 32, LANES), (1, 0))
+    p = turned[pl.ds(pl.multiple_of(x * YL * 8, YL * 8), YL * 8), :]
     mass = jnp.sum(p, axis=1, keepdims=True)
-
     value = jnp.dot(
-        p.astype(BF16), dfull[...], preferred_element_type=F32
+        p.astype(BF16), dfull[...].reshape(C * 32, FS), preferred_element_type=F32
     ) / mass
-    tbuf[...] = value.reshape(X, YL, 8, FQ).astype(BF16)
+    tbuf[...] = value.reshape(YL, 8, FS).astype(BF16)
 
     def send_t(s, carry):
-        t = lax.rem(q + s, Q)
-        pltpu.make_async_remote_copy(
-            tbuf.at[t % X, t // X], out_ref.at[q], os_, or_,
-            device_id=(t * 2 + k, c), device_id_type=MESH,
-        ).start()
-        return carry
-
-    lax.fori_loop(1, Q, send_t, 0)
-    pltpu.make_async_copy(tbuf.at[x, yl], out_ref.at[q], or_).start()
+        t = lax.rem(yl + s, YL)
+        pltpu.make_async_remote_copy(
+            tbuf.at[t], out_ref.at[yl], os_, or_,
+            device_id=(place(t, x, k), c), device_id_type=MESH,
+        ).start()
+        return carry
+
+    lax.fori_loop(1, YL, send_t, 0)
+    pltpu.make_async_copy(tbuf.at[yl], out_ref.at[yl], or_).start()
 
     mine = own_u[:, 0:8]
     for t in range(1, Q):
         mine = jnp.where(x * YL + yl == t, own_u[:, 8 * t:8 * t + 8], mine)
-    npot_ref[...] = mine * eps
+    pots[0:1, 0:8] = mine * eps
     lanes4 = lax.broadcasted_iota(jnp.int32, (X, 8, LANES), 2)
     index4 = lax.broadcasted_iota(jnp.int32, (X, 8, LANES), 0) * 8 + lax.broadcasted_iota(
         jnp.int32, (X, 8, LANES), 1
     )
     block = jnp.where(lanes4 == index4, vbuf[yh, :, z], 0.0)
     block = jnp.sum(jnp.sum(block, axis=0), axis=0, keepdims=True)
-    dpot_ref[...] = block[:, 0:32] * eps
+    pots[1:2, :] = block * eps
+    pltpu.make_async_copy(pots, pots_ref, ps).start()
     finish()
 
 
@@ -483,18 +499,16 @@
     width = noise.shape[1] * C
     FQ = width // (Q * C)
     FS = X * FQ
-    vmem = pl.BlockSpec(memory_space=pltpu.VMEM)
     anywhere = pl.BlockSpec(memory_space=pl.ANY)
     dma = pltpu.SemaphoreType.DMA
-    targets, noise_pot, data_pot = pl.pallas_call(
+    targets, pots = pl.pallas_call(
         functools.partial(kernel, width),
         out_shape=(
-            jax.ShapeDtypeStruct((Q, 8, FQ), BF16),
-            jax.ShapeDtypeStruct((1, 8), F32),
-            jax.ShapeDtypeStruct((1, 32), F32),
+            jax.ShapeDtypeStruct((YL, 8, FS), BF16),
+            jax.ShapeDtypeStruct((2, LANES), F32),
         ),
         in_specs=[anywhere] * 4,
-        out_specs=(anywhere, vmem, vmem),
+        out_specs=(anywhere, anywhere),
         scratch_shapes=[
             pltpu.SMEM((8,), jnp.int32),
             pltpu.SMEM((32,), jnp.int32),
@@ -506,8 +520,8 @@
             pltpu.VMEM((2, X, YL, 8, FS + LANES), BF16),
             pltpu.VMEM((2, 8 * Q, FS + LANES), BF16),
             pltpu.VMEM((Z, X, 8, FQ), BF16),
-            pltpu.VMEM((Z, 2 * X, 8, FQ), BF16),
-            pltpu.VMEM((C * 32, FQ), BF16),
+            pltpu.VMEM((2 * X, Z, X, 8, FQ), BF16),
+            pltpu.VMEM((2 * X, Z * 8, FS), BF16),
             pltpu.VMEM((Z, YH, 1, LANES), F32),
             pltpu.VMEM((Y, 2, 8, LANES), F32),
             pltpu.VMEM((Y, 2, 8, LANES), F32),
@@ -516,16 +530,18 @@
             pltpu.VMEM((2, X, Y, 2, 8, LANES), F32),
             pltpu.VMEM((2, X, Y, 8, LANES), F32),
             pltpu.VMEM((2, X, Y, 8, LANES), F32),
-            pltpu.VMEM((Z, 2, X, 8, LANES), F32),
-            pltpu.VMEM((X, YL, 8, FQ), BF16),
+            pltpu.VMEM((2, X, Z, 8, LANES), F32),
+            pltpu.VMEM((LANES, C * 32), F32),
+            pltpu.VMEM((YL, 8, FS), BF16),
+            pltpu.VMEM((2, LANES), F32),
             dma((3 + YL,)),
-        ] + [dma] * 5 + [dma((Z,))] + [dma] * 8 + [dma((2,))] * 2 + [dma] * 5 + [dma((Y,)), dma, dma((X,)), dma, dma],
+        ] + [dma] * 5 + [dma((Z,))] + [dma] * 8 + [dma((3,))] * 2 + [dma] * 5 + [dma((Y,)), dma, dma((X,)), dma, dma, dma],
         compiler_params=pltpu.CompilerParams(
             collective_id=0, has_side_effects=True, vmem_limit_bytes=60 * 1024 * 1024
         ),
     )(noise_weight, data_weight, noise, data)
-    targets = jnp.transpose(targets, (1, 0, 2)).reshape(8, Q * FQ)
-    return (targets, noise_pot.reshape(8), data_pot.reshape(32))
+    targets = jnp.transpose(targets, (1, 0, 2)).reshape(8, YL * FS)
+    return (targets, pots[0, 0:8], pots[1, 0:32])
 
 
 def solution(mesh):

time: 58.3 us -> 57.2 us (0.981)
  Pallas kernels: 54.9 us -> 53.2 us
    pallas_call x1, Pallas kernels: 54.9 us -> 53.2 us  [per_device(): pl.pallas_call(functools.partial(kernel, width), out_shape=(jax.ShapeDtyp...]
    squeeze x0 -> x2, local copies, waits for them, and re-layouts: none -> 1.02 us  [per_device(): return (targets, pots[0, 0:8], pots[1, 0:32])]
    unnamed x7 -> x3, local copies, waits for them, and re-layouts: 2.59 us -> 2.13 us
where the time goes in v6:
time: 57.2 us; the launch traced here: 57 us
  Pallas kernels  53.2 us (93%)
  local copies, waits for them, and re-layouts  3.15 us (6%)
  between operations  0.65 us (1%)
    pallas_call x1, Pallas kernels, per_device(): pl.pallas_call(functools.partial(kernel, width), out_shape=(jax.ShapeDtyp...  53.2 us
    unnamed x3, local copies, waits for them, and re-layouts  2.13 us

profile of v6, /device:TPU:1, one launch (start us, length us, event | category | flops | bytes accessed | tf_op | source)
XLA Modules:
  0.0 57.0 jit_solution(13131707955973462746)
XLA Ops:
  0.6 53.2 %shard_map.67 = (bf16[4,8,1024]{2,1,0:T(8,128)(2,1)}, f32[2,128]{1,0:T(2,128)}) custom-call(s32[8]{0:T(128)} %nw_hbm.1, s32[32]{0:T(128)} %dw_hbm.1, bf16[8,4096]{1,0:T(8,128)(2,1)} %noise_ref.1, bf16[32,2048]{1,0:T(8,128)(2,1)} %data_ref.1), custom_call_target="tpu_custom_call" | custom-call | tf_op jit(solution)/shard_map/pallas_call | solution.py:504
  53.8 0.0 copy-start
  53.8 0.7 %copy-done = f32[2,128]{1,0:T(2,128)S(1)} copy-done((f32[2,128]{1,0:T(2,128)S(1)}, f32[2,128]{1,0:T(2,128)}, u32[]{:S(2)}) %copy-start) | copy-done | bytes 1048
  54.5 0.5 slice_bitcast_fusion
  55.0 0.5 slice_bitcast_fusion.1
  55.5 1.5 %copy.8 = bf16[8,4096]{1,0:T(8,128)(2,1)} copy(bf16[8,4096]{1,0:T(8,128)(2,1)} %bitcast.7) | data formatting | bytes 131072
Async XLA Ops:
  53.8 0.7 %copy-start = (f32[2,128]{1,0:T(2,128)S(1)}, f32[2,128]{1,0:T(2,128)}, u32[]{:S(2)}) copy-start(f32[2,128]{1,0:T(2,128)} %get-tuple-element.6) | copy-start | bytes 3076

commit v7 on v6

--- a/solution.py
+++ b/solution.py
@@ -23,14 +23,15 @@
 def kernel(
     width,
     nw_hbm, dw_hbm, noise_ref, data_ref,
-    out_ref, pots_ref,
+    out_ref, npot_ref, dpot_ref,
     nw_ref, dw_ref, nstage, dvm, dstage, relay, wstage, nbuf, nmat, dcrit, tdata, dfull,
-    wbuf, pbuf, abuf, bbuf, rbuf, gall, lbuf, vbuf, plan, turned, tbuf, pots,
+    wbuf, pbuf, abuf, bbuf, rbuf, gall, lbuf, vbuf, plan, turned, tbuf, npot, dpot,
     load, n1s, n1r, n2s, n2r, es, er, fs, fr, ts, tr, w1s, w1r, w2s, w2r, sib_s, sib_r,
     as_, ar, bs, br, gs, gr, hs, hr, os_, or_, ps,
 ):
     FQ = width // (Q * C)
     FS = X * FQ
+    FH = FS // YH
     eps = 1.0 / math.sqrt(width)
     row = lax.axis_index("row")
     c = lax.axis_index("col")
@@ -49,13 +50,12 @@
     sibling = (place(yl, x, other), c)
 
     def relay_of(j):
-        return place(2 * k + j // X, j % X, yh), z * YH + x % YH
+        return place(j // X, j % X, yh), z * YH + k
 
     def relay_source(i):
-        f = YH * i + yh
-        return place(f // X, f % X, yl // 2), z * YH + k
-
-    to_self = jnp.logical_and(jnp.logical_and(k == yl // 2, yh == k), x % YH == yh)
+        return i * 2 + yh, z * YH + k
+
+    to_self = k == yh
     n_self = jnp.where(to_self, 1, 0).astype(jnp.int32)
 
     def finish():
@@ -64,14 +64,14 @@
 
         @pl.when(to_self)
         def _():
-            sent(dstage.at[pl.ds(0, 2 * X - 1)], es)
+            sent(dstage.at[pl.ds(0, Q - 1)], es)
 
         @pl.when(jnp.logical_not(to_self))
         def _():
             sent(dstage, es)
 
         sent(relay.at[pl.ds(0, Z - 1)], fs)
-        sent(nstage.at[pl.ds(0, YL - 1)], n1s)
+        sent(nstage.at[pl.ds(0, Y - 1)], n1s)
         sent(nbuf.at[k, pl.ds(0, X - 1)], n2s)
         sent(nbuf.at[k], sib_s.at[0])
         sent(wbuf.at[pl.ds(0, Z - 1), 0], w1s)
@@ -83,9 +83,10 @@
         sent(gall.at[k, pl.ds(0, X - 1)], hs)
         sent(gall.at[k], sib_s.at[1])
         sent(tdata.at[pl.ds(0, X)], sib_s.at[2])
-        sent(out_ref.at[pl.ds(0, YL - 1)], os_)
+        sent(out_ref.at[pl.ds(0, Y - 1)], os_)
         sent(out_ref, or_)
-        sent(pots_ref, ps)
+        sent(npot_ref, ps.at[0])
+        sent(dpot_ref, ps.at[1])
 
     loads = [
         pltpu.make_async_copy(nw_hbm, nw_ref, load.at[0]),
@@ -93,9 +94,9 @@
         pltpu.make_async_copy(data_ref, dvm, load.at[2]),
     ] + [
         pltpu.make_async_copy(
-            noise_ref.at[:, pl.ds(t * FS, FS)], nstage.at[t, :, pl.ds(0, FS)], load.at[3 + t]
+            noise_ref.at[:, pl.ds(t * FH, FH)], nstage.at[t, :, pl.ds(0, FH)], load.at[3 + t]
         )
-        for t in range(YL)
+        for t in range(Y)
     ]
 
     barrier = pltpu.get_barrier_semaphore()
@@ -127,7 +128,7 @@
 
     for copy in loads[2::-1]:
         copy.start()
-    lax.fori_loop(0, Z, greet_source, 0)
+    lax.fori_loop(0, Q, greet_source, 0)
     lax.fori_loop(1, Z, greet_z, 0)
     lax.fori_loop(1, Y, greet_y, 0)
     lax.fori_loop(1, X, greet_x, 0)
@@ -136,12 +137,13 @@
         copy.start()
 
     loads[2].wait()
-    for j in range(2 * X):
+    for j in range(Q):
         s, t = j // X, j % X
-        for f in range(X):
-            cut = dvm[:, s * FS + f * FQ:s * FS + (f + 1) * FQ].astype(F32)
-            dstage[j, f] = cut[8 * t:8 * t + 8].astype(BF16)
-    pl.semaphore_wait(barrier, (Y - 1) + (X - 1) + (Z - 1) + 1 + 2 * X - n_self)
+        for f in range(FH // FQ):
+            at = s * FH + f * FQ
+            dstage[j, f] = dvm[:, at:at + FQ].astype(F32)[8 * t:8 * t + 8].astype(BF16)
+
+    pl.semaphore_wait(barrier, (Y - 1) + (X - 1) + (Z - 1) + 1 + Q - n_self)
 
     def send_data(j, carry):
         device = relay_of(j)
@@ -150,18 +152,18 @@
 
         @pl.when(is_self)
         def _():
-            pltpu.make_async_copy(dstage.at[j], relay.at[slot], er.at[slot]).start()
+            pltpu.make_async_copy(dstage.at[j], relay.at[slot, q % YH], er.at[slot]).start()
 
         @pl.when(jnp.logical_not(is_self))
         def _():
             pltpu.make_async_remote_copy(
-                dstage.at[j], relay.at[slot], es, er.at[slot],
+                dstage.at[j], relay.at[slot, q % YH], es, er.at[slot],
                 device_id=device, device_id_type=MESH,
             ).start()
 
         return carry
 
-    lax.fori_loop(0, 2 * X, send_data, 0)
+    lax.fori_loop(0, Q, send_data, 0)
 
     loads[0].wait()
     for copy in loads[3:]:
@@ -173,8 +175,8 @@
     for i in range(8):
         noise_w = jnp.where(rows8 == i, nw_ref[i], noise_w)
     noise_w = noise_w.astype(F32)
-    for t in range(YL):
-        nf = nstage[t, :, 0:FS].astype(F32)
+    for t in range(Y):
+        nf = nstage[t, :, 0:FH].astype(F32)
         sq = jnp.sum(nf * nf, axis=1, keepdims=True)
         hi = sq.astype(BF16).astype(F32)
         mid = (sq - hi).astype(BF16).astype(F32)
@@ -183,18 +185,21 @@
         tail = jnp.where(lanes8 == 2, lo, tail)
         tail = jnp.where(lanes8 == 1, mid, tail)
         tail = jnp.where(lanes8 == 0, hi, tail)
-        nstage[t, :, FS:FS + LANES] = tail.astype(BF16)
+        nstage[t, :, FH:FH + LANES] = tail.astype(BF16)
+
+    def y_peer(t):
+        return place(t % YL, x, k), z * YH + t // YL
 
     def send_noise_y(s, carry):
-        t = lax.rem(yl + s, YL)
-        pltpu.make_async_remote_copy(
-            nstage.at[t], nbuf.at[k, x, yl], n1s, n1r,
-            device_id=(place(t, x, k), c), device_id_type=MESH,
-        ).start()
-        return carry
-
-    lax.fori_loop(1, YL, send_noise_y, 0)
-    pltpu.make_async_copy(nstage.at[yl], nbuf.at[k, x, yl], n1r).start()
+        t = lax.rem(y + s, Y)
+        pltpu.make_async_remote_copy(
+            nstage.at[t], nbuf.at[k, x, yl, yh], n1s, n1r,
+            device_id=y_peer(t), device_id_type=MESH,
+        ).start()
+        return carry
+
+    lax.fori_loop(1, Y, send_noise_y, 0)
+    pltpu.make_async_copy(nstage.at[y], nbuf.at[k, x, yl, yh], n1r).start()
 
     loads[1].wait()
     lanes1 = lax.broadcasted_iota(jnp.int32, (1, LANES), 1)
@@ -254,9 +259,10 @@
     lax.fori_loop(0, Z, hand_on, 0)
 
     def noise_rows(core):
-        for t in range(2):
-            part = nbuf[core, 2 * t:2 * t + 2].astype(F32)
-            nmat[core, t * 4 * Q:(t + 1) * 4 * Q, :] = part.reshape(4 * Q, FS + LANES).astype(BF16)
+        for t in range(YH):
+            part = nbuf[core, :, :, t].astype(F32).reshape(8 * Q, FH + LANES).astype(BF16)
+            nmat[core, :, t * FH:(t + 1) * FH] = part[:, 0:FH]
+            nmat[core, :, FS + t * LANES:FS + (t + 1) * LANES] = part[:, FH:FH + LANES]
 
     arrived(nbuf.at[k, pl.ds(0, X - 1)], n2r)
     noise_swap = swap(nbuf.at[k], 0)
@@ -264,9 +270,10 @@
     noise_rows(k)
     arrived(nbuf.at[other], sib_r.at[0])
     noise_rows(other)
-    tail = nmat[:, :, FS:FS + LANES].reshape(16 * Q, LANES)
-    pick_sq = jnp.where(lanes8 < 3, 1.0, 0.0).astype(BF16)
-    pick_w = jnp.where(lanes8 == 3, 1.0, 0.0).astype(BF16)
+    tail = nmat[:, :, FS:FS + YH * LANES].reshape(16 * Q, YH * LANES)
+    tail_lane = lax.broadcasted_iota(jnp.int32, (8, YH * LANES), 1)
+    pick_sq = jnp.where(tail_lane % LANES < 3, 1.0, 0.0).astype(BF16)
+    pick_w = jnp.where(tail_lane == 3, 1.0, 0.0).astype(BF16)
     nsq = lax.dot_general(pick_sq, tail, NT, preferred_element_type=F32)[0:1, :]
     wa = lax.dot_general(pick_w, tail, NT, preferred_element_type=F32)[0:1, :]
 
@@ -277,7 +284,7 @@
     ).start()
 
     arrived(dcrit, fr)
-    df = dcrit[...].astype(F32)
+    df = dcrit[...].astype(F32).reshape(Z, X, 8, FQ)
     part = jnp.sum(
         jnp.sum(df * df, axis=1).reshape(Z * 8, FQ), axis=1, keepdims=True
     ) + nsq
@@ -290,9 +297,6 @@
         )
     for h in range(2):
         pbuf[:, h] = part[:, h * LANES:(h + 1) * LANES].reshape(Y, 8, LANES)
-
-    def y_peer(t):
-        return place(t % YL, x, k), z * YH + t // YL
 
     def send_a(s, carry):
         t = lax.rem(y + s, Y)
@@ -375,7 +379,7 @@
         def step(i, carry):
             g = core * X + i
             for f in range(X):
-                cut = tdata[g, :, f].astype(F32).reshape(Z * 8, FQ)
+                cut = tdata[g, :, f // YH, f % YH].astype(F32).reshape(Z * 8, FQ)
                 dfull[g, :, f * FQ:(f + 1) * FQ] = cut.astype(BF16)
             return carry
 
@@ -456,7 +460,6 @@
         for i in range(2 * X):
             peak = data_step(i, peak)
 
-    pots[...] = jnp.zeros_like(pots)
     own_u = jnp.where(k == 0, u[0], u[1])
     for i in range(2 * X):
         a, b = parts(i)
@@ -467,31 +470,33 @@
     value = jnp.dot(
         p.astype(BF16), dfull[...].reshape(C * 32, FS), preferred_element_type=F32
     ) / mass
-    tbuf[...] = value.reshape(YL, 8, FS).astype(BF16)
+    for t in range(YH):
+        tbuf[t] = value[:, t * FH:(t + 1) * FH].reshape(YL, 8, FH).astype(BF16)
 
     def send_t(s, carry):
-        t = lax.rem(yl + s, YL)
-        pltpu.make_async_remote_copy(
-            tbuf.at[t], out_ref.at[yl], os_, or_,
-            device_id=(place(t, x, k), c), device_id_type=MESH,
-        ).start()
-        return carry
-
-    lax.fori_loop(1, YL, send_t, 0)
-    pltpu.make_async_copy(tbuf.at[yl], out_ref.at[yl], or_).start()
+        t = lax.rem(y + s, Y)
+        pltpu.make_async_remote_copy(
+            tbuf.at[t // YL, t % YL], out_ref.at[y], os_, or_,
+            device_id=y_peer(t), device_id_type=MESH,
+        ).start()
+        return carry
+
+    lax.fori_loop(1, Y, send_t, 0)
+    pltpu.make_async_copy(tbuf.at[yh, yl], out_ref.at[y], or_).start()
 
     mine = own_u[:, 0:8]
     for t in range(1, Q):
         mine = jnp.where(x * YL + yl == t, own_u[:, 8 * t:8 * t + 8], mine)
-    pots[0:1, 0:8] = mine * eps
+    npot[...] = mine * eps
     lanes4 = lax.broadcasted_iota(jnp.int32, (X, 8, LANES), 2)
     index4 = lax.broadcasted_iota(jnp.int32, (X, 8, LANES), 0) * 8 + lax.broadcasted_iota(
         jnp.int32, (X, 8, LANES), 1
     )
     block = jnp.where(lanes4 == index4, vbuf[yh, :, z], 0.0)
     block = jnp.sum(jnp.sum(block, axis=0), axis=0, keepdims=True)
-    pots[1:2, :] = block * eps
-    pltpu.make_async_copy(pots, pots_ref, ps).start()
+    dpot[...] = block[:, 0:32] * eps
+    pltpu.make_async_copy(npot, npot_ref, ps.at[0]).start()
+    pltpu.make_async_copy(dpot, dpot_ref, ps.at[1]).start()
     finish()
 
 
@@ -501,26 +506,27 @@
     FS = X * FQ
     anywhere = pl.BlockSpec(memory_space=pl.ANY)
     dma = pltpu.SemaphoreType.DMA
-    targets, pots = pl.pallas_call(
+    targets, noise_pot, data_pot = pl.pallas_call(
         functools.partial(kernel, width),
         out_shape=(
-            jax.ShapeDtypeStruct((YL, 8, FS), BF16),
-            jax.ShapeDtypeStruct((2, LANES), F32),
+            jax.ShapeDtypeStruct((Y, 8, FS // YH), BF16),
+            jax.ShapeDtypeStruct((1, 8), F32),
+            jax.ShapeDtypeStruct((1, 32), F32),
         ),
         in_specs=[anywhere] * 4,
-        out_specs=(anywhere, anywhere),
+        out_specs=(anywhere, anywhere, anywhere),
         scratch_shapes=[
             pltpu.SMEM((8,), jnp.int32),
             pltpu.SMEM((32,), jnp.int32),
-            pltpu.VMEM((YL, 8, FS + LANES), BF16),
+            pltpu.VMEM((Y, 8, FS // YH + LANES), BF16),
             pltpu.VMEM((32, 2 * FS), BF16),
-            pltpu.VMEM((2 * X, X, 8, FQ), BF16),
-            pltpu.VMEM((Z, X, 8, FQ), BF16),
+            pltpu.VMEM((Q, X // YH, 8, FQ), BF16),
+            pltpu.VMEM((Z, YH, X // YH, 8, FQ), BF16),
             pltpu.VMEM((1, LANES), F32),
-            pltpu.VMEM((2, X, YL, 8, FS + LANES), BF16),
-            pltpu.VMEM((2, 8 * Q, FS + LANES), BF16),
-            pltpu.VMEM((Z, X, 8, FQ), BF16),
-            pltpu.VMEM((2 * X, Z, X, 8, FQ), BF16),
+            pltpu.VMEM((2, X, YL, YH, 8, FS // YH + LANES), BF16),
+            pltpu.VMEM((2, 8 * Q, FS + YH * LANES), BF16),
+            pltpu.VMEM((Z, YH, X // YH, 8, FQ), BF16),
+            pltpu.VMEM((2 * X, Z, YH, X // YH, 8, FQ), BF16),
             pltpu.VMEM((2 * X, Z * 8, FS), BF16),
             pltpu.VMEM((Z, YH, 1, LANES), F32),
             pltpu.VMEM((Y, 2, 8, LANES), F32),
@@ -532,16 +538,17 @@
             pltpu.VMEM((2, X, Y, 8, LANES), F32),
             pltpu.VMEM((2, X, Z, 8, LANES), F32),
             pltpu.VMEM((LANES, C * 32), F32),
-            pltpu.VMEM((YL, 8, FS), BF16),
-            pltpu.VMEM((2, LANES), F32),
-            dma((3 + YL,)),
-        ] + [dma] * 5 + [dma((Z,))] + [dma] * 8 + [dma((3,))] * 2 + [dma] * 5 + [dma((Y,)), dma, dma((X,)), dma, dma, dma],
+            pltpu.VMEM((YH, YL, 8, FS // YH), BF16),
+            pltpu.VMEM((1, 8), F32),
+            pltpu.VMEM((1, 32), F32),
+            dma((3 + Y,)),
+        ] + [dma] * 5 + [dma((Z,))] + [dma] * 8 + [dma((3,))] * 2 + [dma] * 5 + [dma((Y,)), dma, dma((X,)), dma, dma, dma((2,))],
         compiler_params=pltpu.CompilerParams(
             collective_id=0, has_side_effects=True, vmem_limit_bytes=60 * 1024 * 1024
         ),
     )(noise_weight, data_weight, noise, data)
     targets = jnp.transpose(targets, (1, 0, 2)).reshape(8, YL * FS)
-    return (targets, pots[0, 0:8], pots[1, 0:32])
+    return (targets, noise_pot.reshape(8), data_pot.reshape(32))
 
 
 def solution(mesh):

time: 57.2 us -> 59.7 us (1.044)
  Pallas kernels: 53.2 us -> 56.2 us
    pallas_call x1, Pallas kernels: 53.2 us -> 56.2 us  [per_device(): pl.pallas_call(functools.partial(kernel, width), out_shape=(jax.ShapeDtyp...]
    squeeze x2 -> x0, local copies, waits for them, and re-layouts: 1.02 us -> none  [per_device(): return (targets, pots[0, 0:8], pots[1, 0:32])]
    unnamed x3 -> x7, local copies, waits for them, and re-layouts: 2.13 us -> 2.59 us
where the time goes in v7:
time: 59.7 us; the launch traced here: 59.5 us
  Pallas kernels  56.2 us (94%)
  local copies, waits for them, and re-layouts  2.59 us (4%)
  between operations  0.65 us (1%)
    pallas_call x1, Pallas kernels, per_device(): pl.pallas_call(functools.partial(kernel, width), out_shape=(jax.ShapeDtyp...  56.2 us
    unnamed x7, local copies, waits for them, and re-layouts  2.59 us

profile of v7, /device:TPU:1, one launch (start us, length us, event | category | flops | bytes accessed | tf_op | source)
XLA Modules:
  0.0 59.5 jit_solution(5478165534338242521)
XLA Ops:
  0.6 56.2 %shard_map.67 = (bf16[8,8,512]{2,1,0:T(8,128)(2,1)}, f32[1,8]{1,0:T(1,128)}, f32[1,32]{1,0:T(1,128)}) custom-call(s32[8]{0:T(128)} %nw_hbm.1, s32[32]{0:T(128)} %dw_hbm.1, bf16[8,4096]{1,0:T(8,128)(2,1)} %noise_ref.1, bf16[32,2048]{1,0:T(8,128)(2,1)} %data_ref.1), custom_call_target="tpu_custom_call" | custom-call | tf_op jit(solution)/shard_map/pallas_call | solution.py:509
  56.9 0.0 copy-start.1
  56.9 1.5 %copy.10 = bf16[8,4096]{1,0:T(8,128)(2,1)} copy(bf16[8,4096]{1,0:T(8,128)(2,1)} %bitcast.5) | data formatting | bytes 131072
  58.4 0.0 copy-done.1
  58.4 0.0 copy-start
  58.4 0.5 copy.11
  58.9 0.1 copy-done
  59.0 0.5 copy.12
Async XLA Ops:
  56.9 1.5 %copy-start.1 = (f32[1,8]{1,0:T(1,128)S(1)}, f32[1,8]{1,0:T(1,128)}, u32[]{:S(2)}) copy-start(f32[1,8]{1,0:T(1,128)} %get-tuple-element.7) | copy-start | bytes 100
  58.4 0.6 %copy-start = (f32[1,32]{1,0:T(1,128)S(1)}, f32[1,32]{1,0:T(1,128)}, u32[]{:S(2)}) copy-start(f32[1,32]{1,0:T(1,128)} %get-tuple-element.8) | copy-start | bytes 388

commit v8 on v6

--- a/solution.py
+++ b/solution.py
@@ -23,9 +23,9 @@
 def kernel(
     width,
     nw_hbm, dw_hbm, noise_ref, data_ref,
-    out_ref, pots_ref,
+    out_ref, npot_ref, dpot_ref,
     nw_ref, dw_ref, nstage, dvm, dstage, relay, wstage, nbuf, nmat, dcrit, tdata, dfull,
-    wbuf, pbuf, abuf, bbuf, rbuf, gall, lbuf, vbuf, plan, turned, tbuf, pots,
+    wbuf, pbuf, abuf, bbuf, rbuf, gall, lbuf, vbuf, plan, turned, tbuf, npot, dpot,
     load, n1s, n1r, n2s, n2r, es, er, fs, fr, ts, tr, w1s, w1r, w2s, w2r, sib_s, sib_r,
     as_, ar, bs, br, gs, gr, hs, hr, os_, or_, ps,
 ):
@@ -85,7 +85,8 @@
         sent(tdata.at[pl.ds(0, X)], sib_s.at[2])
         sent(out_ref.at[pl.ds(0, YL - 1)], os_)
         sent(out_ref, or_)
-        sent(pots_ref, ps)
+        sent(npot_ref, ps.at[0])
+        sent(dpot_ref, ps.at[1])
 
     loads = [
         pltpu.make_async_copy(nw_hbm, nw_ref, load.at[0]),
@@ -456,7 +457,6 @@
         for i in range(2 * X):
             peak = data_step(i, peak)
 
-    pots[...] = jnp.zeros_like(pots)
     own_u = jnp.where(k == 0, u[0], u[1])
     for i in range(2 * X):
         a, b = parts(i)
@@ -483,16 +483,36 @@
     mine = own_u[:, 0:8]
     for t in range(1, Q):
         mine = jnp.where(x * YL + yl == t, own_u[:, 8 * t:8 * t + 8], mine)
-    pots[0:1, 0:8] = mine * eps
+    npot[...] = mine * eps
     lanes4 = lax.broadcasted_iota(jnp.int32, (X, 8, LANES), 2)
     index4 = lax.broadcasted_iota(jnp.int32, (X, 8, LANES), 0) * 8 + lax.broadcasted_iota(
         jnp.int32, (X, 8, LANES), 1
     )
     block = jnp.where(lanes4 == index4, vbuf[yh, :, z], 0.0)
     block = jnp.sum(jnp.sum(block, axis=0), axis=0, keepdims=True)
-    pots[1:2, :] = block * eps
-    pltpu.make_async_copy(pots, pots_ref, ps).start()
+    dpot[...] = block[:, 0:32] * eps
+    pltpu.make_async_copy(npot, npot_ref, ps.at[0]).start()
+    pltpu.make_async_copy(dpot, dpot_ref, ps.at[1]).start()
     finish()
+
+
+def leave(targets_ref, npot_ref, dpot_ref, out_ref, nout_ref, dout_ref, held, npot, dpot, into, out):
+    width = targets_ref.shape[2]
+    sources = [npot_ref, dpot_ref] + [targets_ref.at[t] for t in range(YL)]
+    places = [npot, dpot] + [held.at[t] for t in range(YL)]
+    results = [nout_ref, dout_ref] + [
+        out_ref.at[:, pl.ds(t * width, width)] for t in range(YL)
+    ]
+    count = len(places)
+    first = [pltpu.make_async_copy(sources[i], places[i], into.at[i]) for i in range(count)]
+    second = [pltpu.make_async_copy(places[i], results[i], out.at[i]) for i in range(count)]
+    for copy in first:
+        copy.start()
+    for i in range(count):
+        first[i].wait()
+        second[i].start()
+    for copy in second:
+        copy.wait()
 
 
 def per_device(noise, data, noise_weight, data_weight):
@@ -501,14 +521,15 @@
     FS = X * FQ
     anywhere = pl.BlockSpec(memory_space=pl.ANY)
     dma = pltpu.SemaphoreType.DMA
-    targets, pots = pl.pallas_call(
+    targets, noise_pot, data_pot = pl.pallas_call(
         functools.partial(kernel, width),
         out_shape=(
             jax.ShapeDtypeStruct((YL, 8, FS), BF16),
-            jax.ShapeDtypeStruct((2, LANES), F32),
+            jax.ShapeDtypeStruct((1, 8), F32),
+            jax.ShapeDtypeStruct((1, 32), F32),
         ),
         in_specs=[anywhere] * 4,
-        out_specs=(anywhere, anywhere),
+        out_specs=(anywhere, anywhere, anywhere),
         scratch_shapes=[
             pltpu.SMEM((8,), jnp.int32),
             pltpu.SMEM((32,), jnp.int32),
@@ -533,15 +554,33 @@
             pltpu.VMEM((2, X, Z, 8, LANES), F32),
             pltpu.VMEM((LANES, C * 32), F32),
             pltpu.VMEM((YL, 8, FS), BF16),
-            pltpu.VMEM((2, LANES), F32),
+            pltpu.VMEM((1, 8), F32),
+            pltpu.VMEM((1, 32), F32),
             dma((3 + YL,)),
-        ] + [dma] * 5 + [dma((Z,))] + [dma] * 8 + [dma((3,))] * 2 + [dma] * 5 + [dma((Y,)), dma, dma((X,)), dma, dma, dma],
+        ] + [dma] * 5 + [dma((Z,))] + [dma] * 8 + [dma((3,))] * 2 + [dma] * 5 + [dma((Y,)), dma, dma((X,)), dma, dma, dma((2,))],
         compiler_params=pltpu.CompilerParams(
             collective_id=0, has_side_effects=True, vmem_limit_bytes=60 * 1024 * 1024
         ),
     )(noise_weight, data_weight, noise, data)
-    targets = jnp.transpose(targets, (1, 0, 2)).reshape(8, YL * FS)
-    return (targets, pots[0, 0:8], pots[1, 0:32])
+    targets, noise_pot, data_pot = pl.pallas_call(
+        leave,
+        out_shape=(
+            jax.ShapeDtypeStruct((8, YL * FS), BF16),
+            jax.ShapeDtypeStruct((1, 8), F32),
+            jax.ShapeDtypeStruct((1, 32), F32),
+        ),
+        in_specs=[anywhere] * 3,
+        out_specs=(anywhere, anywhere, anywhere),
+        scratch_shapes=[
+            pltpu.VMEM((YL, 8, FS), BF16),
+            pltpu.VMEM((1, 8), F32),
+            pltpu.VMEM((1, 32), F32),
+            dma((YL + 2,)),
+            dma((YL + 2,)),
+        ],
+        compiler_params=pltpu.CompilerParams(vmem_limit_bytes=60 * 1024 * 1024),
+    )(targets, noise_pot, data_pot)
+    return (targets, noise_pot.reshape(8), data_pot.reshape(32))
 
 
 def solution(mesh):

time: 57.2 us -> 55.5 us (0.970)
  local copies, waits for them, and re-layouts: 3.15 us -> 0 us
  Pallas kernels: 53.2 us -> 54.7 us
    unnamed x3 -> x0, local copies, waits for them, and re-layouts: 2.13 us -> none
    pallas_call x0 -> x1, Pallas kernels: none -> 1.49 us  [per_device(): pl.pallas_call(leave, out_shape=(jax.ShapeDtypeStruct((8, YL * FS), BF16)...]
    squeeze x2 -> x0, local copies, waits for them, and re-layouts: 1.02 us -> none  [per_device(): return (targets, pots[0, 0:8], pots[1, 0:32])]
where the time goes in v8:
time: 55.5 us; the launch traced here: 55.3 us
  Pallas kernels  54.7 us (99%)
  between operations  0.64 us (1%)
    pallas_call x1, Pallas kernels, per_device(): pl.pallas_call(functools.partial(kernel, width), out_shape=(jax.ShapeDtyp...  53.2 us
    pallas_call x1, Pallas kernels, per_device(): pl.pallas_call(leave, out_shape=(jax.ShapeDtypeStruct((8, YL * FS), BF16)...  1.49 us

profile of v8, /device:TPU:1, one launch (start us, length us, event | category | flops | bytes accessed | tf_op | source)
XLA Modules:
  0.0 55.3 jit_solution(6546133865987292407)
XLA Ops:
  0.6 53.2 %shard_map.67 = (bf16[4,8,1024]{2,1,0:T(8,128)(2,1)}, f32[1,8]{1,0:T(1,128)}, f32[1,32]{1,0:T(1,128)}) custom-call(s32[8]{0:T(128)} %nw_hbm.1, s32[32]{0:T(128)} %dw_hbm.1, bf16[8,4096]{1,0:T(8,128)(2,1)} %noise_ref.1, bf16[32,2048]{1,0:T(8,128)(2,1)} %data_ref.1), custom_call_target="tpu_custom_call" | custom-call | tf_op jit(solution)/shard_map/pallas_call | solution.py:524
  53.8 1.5 %shard_map.68 = (bf16[8,4096]{1,0:T(8,128)(2,1)}, f32[1,8]{1,0:T(1,128)}, f32[1,32]{1,0:T(1,128)}) custom-call(bf16[4,8,1024]{2,1,0:T(8,128)(2,1)} %get-tuple-element.9.targets_ref, f32[1,8]{1,0:T(1,128)} %get-tuple-element.10.npot_ref, f32[1,32]{1,0:T(1,128)} %get-tuple-element.11.dpot_ref), custom_call_target="tpu_custom_call" | custom-call | tf_op jit(solution)/shard_map/pallas_call | solution.py:565

commit v9 on v8

--- a/solution.py
+++ b/solution.py
@@ -144,7 +144,8 @@
             dstage[j, f] = cut[8 * t:8 * t + 8].astype(BF16)
     pl.semaphore_wait(barrier, (Y - 1) + (X - 1) + (Z - 1) + 1 + 2 * X - n_self)
 
-    def send_data(j, carry):
+    def send_data(i, carry):
+        j = i // X * X + lax.rem(x + 2 + i, X)
         device = relay_of(j)
         is_self = jnp.logical_and(device[0] == row, device[1] == c)
         slot = q // YH
@@ -215,6 +216,10 @@
     lax.fori_loop(1, Z, send_w, 0)
     pltpu.make_async_copy(wstage, wbuf.at[z, yh], w1r).start()
 
+    def far_first(s, count):
+        d = s // 2
+        return count // 2 + jnp.where(s % 2 == 1, d, -d)
+
     def arrived(ref, sem):
         pltpu.make_async_copy(ref, ref, sem).wait()
 
@@ -296,7 +301,7 @@
         return place(t % YL, x, k), z * YH + t // YL
 
     def send_a(s, carry):
-        t = lax.rem(y + s, Y)
+        t = lax.rem(y + far_first(s, Y), Y)
         pltpu.make_async_remote_copy(
             pbuf.at[t], abuf.at[y], as_, ar, device_id=y_peer(t), device_id_type=MESH
         ).start()
@@ -325,7 +330,7 @@
     bbuf[...] = total
 
     def send_b(s, carry):
-        t = lax.rem(z + s, Z)
+        t = lax.rem(z + far_first(s, Z), Z)
         pltpu.make_async_remote_copy(
             bbuf, rbuf.at[z], bs, br, device_id=(row, t * YH + yh), device_id_type=MESH
         ).start()
@@ -341,7 +346,7 @@
     gall[k, x, y] = total * (-1.0 / (width * eps))
 
     def send_g(s, carry):
-        t = lax.rem(y + s, Y)
+        t = lax.rem(y + far_first(s, Y), Y)
         pltpu.make_async_remote_copy(
             gall.at[k, x, y], gall.at[k, x, y], gs, gr.at[y],
             device_id=y_peer(t), device_id_type=MESH,

time: 55.5 us -> 55.3 us (level)
  no operation moved by 1% of the time
where the time goes in v9:
time: 55.3 us; the launch traced here: 55.1 us
  Pallas kernels  54.4 us (98%)
  between operations  0.64 us (1%)
    pallas_call x1, Pallas kernels, per_device(): pl.pallas_call(functools.partial(kernel, width), out_shape=(jax.ShapeDtyp...  53 us
    pallas_call x1, Pallas kernels, per_device(): pl.pallas_call(leave, out_shape=(jax.ShapeDtypeStruct((8, YL * FS), BF16)...  1.49 us

profile of v9, /device:TPU:1, one launch (start us, length us, event | category | flops | bytes accessed | tf_op | source)
XLA Modules:
  0.0 55.1 jit_solution(8074009887047977109)
XLA Ops:
  0.6 53.0 %shard_map.67 = (bf16[4,8,1024]{2,1,0:T(8,128)(2,1)}, f32[1,8]{1,0:T(1,128)}, f32[1,32]{1,0:T(1,128)}) custom-call(s32[8]{0:T(128)} %nw_hbm.1, s32[32]{0:T(128)} %dw_hbm.1, bf16[8,4096]{1,0:T(8,128)(2,1)} %noise_ref.1, bf16[32,2048]{1,0:T(8,128)(2,1)} %data_ref.1), custom_call_target="tpu_custom_call" | custom-call | tf_op jit(solution)/shard_map/pallas_call | solution.py:529
  53.6 1.5 %shard_map.68 = (bf16[8,4096]{1,0:T(8,128)(2,1)}, f32[1,8]{1,0:T(1,128)}, f32[1,32]{1,0:T(1,128)}) custom-call(bf16[4,8,1024]{2,1,0:T(8,128)(2,1)} %get-tuple-element.9.targets_ref, f32[1,8]{1,0:T(1,128)} %get-tuple-element.10.npot_ref, f32[1,32]{1,0:T(1,128)} %get-tuple-element.11.dpot_ref), custom_call_target="tpu_custom_call" | custom-call | tf_op jit(solution)/shard_map/pallas_call | solution.py:570

commit v10 on v9

--- a/solution.py
+++ b/solution.py
@@ -114,11 +114,11 @@
         return carry
 
     def greet_z(s, carry):
-        greet((row, lax.rem(z + s, Z) * YH + yh))
+        greet((row, lax.rem(z + lax.rem(s + 2, Z - 1) + 1, Z) * YH + yh))
         return carry
 
     def greet_y(s, carry):
-        t = lax.rem(y + s, Y)
+        t = lax.rem(y + lax.rem(s + 2, Y - 1) + 1, Y)
         greet((place(t % YL, x, k), z * YH + t // YL))
         return carry
 

time: 55.3 us -> 55.4 us (level)
  no operation moved by 1% of the time
where the time goes in v10:
time: 55.4 us; the launch traced here: 55.2 us
  Pallas kernels  54.5 us (98%)
  between operations  0.64 us (1%)
    pallas_call x1, Pallas kernels, per_device(): pl.pallas_call(functools.partial(kernel, width), out_shape=(jax.ShapeDtyp...  53 us
    pallas_call x1, Pallas kernels, per_device(): pl.pallas_call(leave, out_shape=(jax.ShapeDtypeStruct((8, YL * FS), BF16)...  1.49 us

profile of v10, /device:TPU:1, one launch (start us, length us, event | category | flops | bytes accessed | tf_op | source)
XLA Modules:
  0.0 55.2 jit_solution(11879808334799706820)
XLA Ops:
  0.6 53.0 %shard_map.67 = (bf16[4,8,1024]{2,1,0:T(8,128)(2,1)}, f32[1,8]{1,0:T(1,128)}, f32[1,32]{1,0:T(1,128)}) custom-call(s32[8]{0:T(128)} %nw_hbm.1, s32[32]{0:T(128)} %dw_hbm.1, bf16[8,4096]{1,0:T(8,128)(2,1)} %noise_ref.1, bf16[32,2048]{1,0:T(8,128)(2,1)} %data_ref.1), custom_call_target="tpu_custom_call" | custom-call | tf_op jit(solution)/shard_map/pallas_call | solution.py:529
  53.7 1.5 %shard_map.68 = (bf16[8,4096]{1,0:T(8,128)(2,1)}, f32[1,8]{1,0:T(1,128)}, f32[1,32]{1,0:T(1,128)}) custom-call(bf16[4,8,1024]{2,1,0:T(8,128)(2,1)} %get-tuple-element.9.targets_ref, f32[1,8]{1,0:T(1,128)} %get-tuple-element.10.npot_ref, f32[1,32]{1,0:T(1,128)} %get-tuple-element.11.dpot_ref), custom_call_target="tpu_custom_call" | custom-call | tf_op jit(solution)/shard_map/pallas_call | solution.py:570
